TPU v7x, 256 devices: a whole 4x4x8 slice. The times are simulated.
256 devices in a mesh: band: 32 (over z_hi, y, core), grid: 8 (over z_lo, x).
Axes of the slice: x: 4, y: 4, z: 8 (z_hi: 4, z_lo: 2; z = z_hi * 2 + z_lo), core: 2. Of those that a mesh axis runs over, the one named last changes fastest.
Arguments:
- block_coeffs: float32 [256, 32768], P('band', 'grid'), may hold values from -6 to 6
- potential: float32 [96, 9216], P('grid'), may hold values from -4 to 4
- lower_edge: float32 [1], replicated, may hold values from 0.8 to 1.2
- upper_edge: float32 [1], replicated, may hold values from 4.5 to 5.5
- rotation: float32 [8, 6144, 8], P(None, 'band'), may hold values from -0.75 to 0.75
- owners: int32 [8], replicated, may hold values from 0 to 31
Outputs:
- filtered: float32 [256, 32768], P('band', 'grid')
- residents: float32 [6144, 32768], P('band', 'grid')
All inputs are finite; a program needn't handle non-finite values.
Results may differ from a plain program's by a relative error of at most 0.000071.
Values sent between devices are 32-bit elements; how exact they have to be, the bound alone decides.
A program may use at most 64 MiB of HBM per device.

v0:
```python
import jax
import jax.numpy as jnp
from jax import lax
from jax.sharding import PartitionSpec as P

NG = 96
KEEP = 32


edge_energy = 1.3


def spread(x, axis, root):
    mine = lax.axis_index(axis) == root
    return lax.psum(jnp.where(mine, x, jnp.zeros_like(x)), axis)


def kept_frequency(kept_count, grid_points):
    ordinal = jnp.arange(kept_count, dtype=jnp.int32)
    return jnp.where(ordinal < kept_count // 2, ordinal, ordinal + (grid_points - kept_count))


def hartley_table(kept_count, grid_points):
    points = jnp.arange(grid_points, dtype=jnp.int32)
    phase_turns = points[:, None] * kept_frequency(kept_count, grid_points)[None, :] % grid_points
    angles = phase_turns.astype(jnp.float32) * (2.0 * jnp.pi / grid_points)
    return (jnp.cos(angles) + jnp.sin(angles)) / jnp.sqrt(jnp.float32(grid_points))


def signed_square(kept_count):
    ordinal = jnp.arange(kept_count, dtype=jnp.int32)
    signed = jnp.where(ordinal < kept_count // 2, ordinal, ordinal - kept_count).astype(jnp.float32)
    return signed * signed / jnp.float32((kept_count // 2) ** 2)


def to_real(coeffs, hartley, potential, keep_local):
    bands_now = coeffs.shape[0]
    coef_cube = coeffs.reshape(bands_now, keep_local, KEEP, KEEP)
    along_x = jnp.einsum("bqkz,nk->bqnz", coef_cube, hartley, precision=lax.Precision.HIGHEST)

    def finish(received):
        along_y = jnp.einsum("bqnz,yq->bnyz", received, hartley, precision=lax.Precision.HIGHEST)
        real_field = jnp.einsum("bnyz,wz->bnyw", along_y, hartley, precision=lax.Precision.HIGHEST)
        planes = real_field.reshape(received.shape[0], potential.shape[0], NG * NG)
        return planes * potential[None]

    return finish(lax.all_to_all(along_x, "grid", split_axis=2, concat_axis=1, tiled=True))


def to_plane(product, hartley, planes_local):
    bands_now = product.shape[0]
    real_field = product.reshape(bands_now, planes_local, NG, NG)
    along_z = jnp.einsum("bnyw,wz->bnyz", real_field, hartley, precision=lax.Precision.HIGHEST)
    along_y = jnp.einsum("bnyz,yq->bqnz", along_z, hartley, precision=lax.Precision.HIGHEST)

    def finish(received):
        along_x = jnp.einsum("bqnz,nk->bqkz", received, hartley, precision=lax.Precision.HIGHEST)
        return along_x.reshape(received.shape[0], -1)

    return finish(lax.all_to_all(along_y, "grid", split_axis=1, concat_axis=2, tiled=True))


def body(block_coeffs, potential, lower_edge, upper_edge, rotation, owners):
    slices = lax.axis_size("grid")
    keep_local = KEEP // slices
    planes_local = potential.shape[0]
    hartley = hartley_table(KEEP, NG)
    square = signed_square(KEEP)
    kinetic_full = edge_energy * (
        square[:, None, None] + square[None, :, None] + square[None, None, :]
    )
    kinetic_rows = kinetic_full.reshape(KEEP, KEEP * KEEP)
    kinetic = lax.dynamic_slice_in_dim(
        kinetic_rows, lax.axis_index("grid") * keep_local, keep_local, 0
    ).reshape(1, -1)
    center = (lower_edge[0] + upper_edge[0]) * 0.5
    half_width = (upper_edge[0] - lower_edge[0]) * 0.5

    def hamiltonian(coeffs):
        product = to_real(coeffs, hartley, potential, keep_local)
        return kinetic * coeffs + to_plane(product, hartley, planes_local)

    first_term = (hamiltonian(block_coeffs) - center * block_coeffs) / half_width
    filtered = 2.0 * (hamiltonian(first_term) - center * first_term) / half_width - block_coeffs
    rotated = jnp.zeros((rotation.shape[1], filtered.shape[1]), jnp.float32)
    for step_index in range(rotation.shape[0]):
        arrived = spread(filtered, "band", owners[step_index])
        rotated = rotated + jnp.dot(
            rotation[step_index],
            arrived,
            precision=lax.Precision.HIGHEST,
            preferred_element_type=jnp.float32,
        )
    return (filtered, rotated)


def solution(mesh):
    return jax.shard_map(
        body,
        mesh=mesh,
        in_specs=(P("band", "grid"), P("grid", None), P(), P(), P(None, "band", None), P()),
        out_specs=(P("band", "grid"), P("band", "grid")),
        check_vma=False,
    )
```

profile of v0, /device:TPU:1, one launch (start us, length us, event | category | flops | bytes accessed | tf_op | source)
XLA Modules:
  0.0 460.5 jit_solution(1405846070344206644)
XLA Ops:
  7.2 1.1 reshape.110
  8.3 1.0 convolution_bitcast_fusion.3
  9.3 1.2 copy.39
  10.5 1.8 reshape.119
  12.3 6.4 %all-to-all-start = ((f32[8,1,12288]{2,1,0:T(1,128)}), f32[8,1,12288]{2,1,0:T(1,128)S(1)}, u32[]{:S(2)}, u32[]{:S(2)}) async-start(f32[8,1,12288]{2,1,0:T(1,128)} %reshape.119), calls=%async_computation | async-start | bytes 786432 | tf_op jit(solution)/shard_map/all_to_all | solution.py:47
  18.6 1.1 mul.206
  19.7 5.6 %all-to-all-done = f32[8,1,12288]{2,1,0:T(1,128)S(1)} async-done(((f32[8,1,12288]{2,1,0:T(1,128)}), f32[8,1,12288]{2,1,0:T(1,128)S(1)}, u32[]{:S(2)}, u32[]{:S(2)}) %all-to-all-start) | async-done | bytes 393248 | tf_op jit(solution)/shard_map/all_to_all | solution.py:47
  25.9 1.6 reduce
  27.5 0.8 reshape.120
  28.5 0.9 copy.42
  29.4 1.6 fusion.54
  31.0 7.8 %fusion.30 = f32[8,12,96,96]{3,2,1,0:T(8,128)S(1)} fusion(f32[8,12,96,32]{2,3,1,0:T(8,128)S(1)} %bitcast.151, s32[32]{0:T(128)S(1)} %compare_select_fusion), kind=kOutput, calls=%fused_computation.50 | convolution fusion | flops 339772416 | bytes 4718720 | tf_op jit(solution)/shard_map/bnyz,wz->bnyw/dot_general | solution.py:43
  38.8 9.8 %fusion.3 = f32[8,12,96,32]{2,3,1,0:T(8,128)S(1)} fusion(f32[8,12,96,96]{3,2,1,0:T(8,128)S(1)} %fusion.30, f32[12,96,96]{2,1,0:T(8,128)S(1)} %copy-done, s32[32]{0:T(128)S(1)} %compare_select_fusion), kind=kOutput, calls=%fused_computation.10 | convolution fusion | flops 340657152 | bytes 5161088 | tf_op jit(solution)/shard_map/bnyw,wz->bnyz/dot_general | solution.py:53
  48.6 7.3 %convolution_bitcast_fusion.1 = f32[8,32,12,32]{3,1,2,0:T(8,128)S(1)} fusion(f32[8,12,96,32]{2,3,1,0:T(8,128)S(1)} %fusion.3, s32[32]{0:T(128)S(1)} %compare_select_fusion), kind=kOutput, calls=%fused_computation.19 | convolution fusion | flops 113280000 | bytes 1572992 | tf_op jit(solution)/shard_map/bnyz,yq->bqnz/dot_general | solution.py:54
  55.9 1.3 copy.71
  57.2 1.4 reshape.121
  58.7 4.5 all-to-all-start.1
  65.1 4.7 %all-to-all-done.1 = f32[8,1,12288]{2,1,0:T(1,128)S(1)} async-done(((f32[8,1,12288]{2,1,0:T(1,128)}), f32[8,1,12288]{2,1,0:T(1,128)S(1)}, u32[]{:S(2)}, u32[]{:S(2)}) %all-to-all-start.1) | async-done | bytes 393248 | tf_op jit(solution)/shard_map/all_to_all | solution.py:60
  69.8 1.6 reduce.1
  72.1 1.3 fusion.11
  73.8 1.0 convolution_bitcast_fusion.2
  74.8 1.2 copy.47
  76.0 1.0 reshape.123
  77.1 9.4 %all_to_all.72 = f32[8,1,12288]{2,1,0:T(1,128)S(1)} all-to-all(f32[8,1,12288]{2,1,0:T(1,128)S(1)} %reshape.123), channel_id=1, replica_groups=mesh['band'=32,'grid'=8] {'grid'}, dimensions={0} | all-to-all | bytes 786432 | tf_op jit(solution)/shard_map/all_to_all | solution.py:47
  86.5 1.6 reduce.2
  88.1 0.8 reshape.124
  89.2 0.9 copy.50
  90.0 1.6 fusion.53
  91.6 8.0 %fusion.24 = f32[8,12,96,96]{3,2,1,0:T(8,128)S(1)} fusion(f32[8,12,96,32]{2,3,1,0:T(8,128)S(1)} %bitcast.153, s32[32]{0:T(128)S(1)} %compare_select_fusion), kind=kOutput, calls=%fused_computation.44 | convolution fusion | flops 339772416 | bytes 4718720 | tf_op jit(solution)/shard_map/bnyz,wz->bnyw/dot_general | solution.py:43
  99.6 9.8 %fusion.1 = f32[8,12,96,32]{2,3,1,0:T(8,128)S(1)} fusion(f32[8,12,96,96]{3,2,1,0:T(8,128)S(1)} %fusion.24, f32[12,96,96]{2,1,0:T(8,128)S(1)} %copy-done.1, s32[32]{0:T(128)S(1)} %compare_select_fusion), kind=kOutput, calls=%fused_computation.8 | convolution fusion | flops 340657152 | bytes 5161088 | tf_op jit(solution)/shard_map/bnyw,wz->bnyz/dot_general | solution.py:53
  109.4 7.3 %convolution_bitcast_fusion = f32[8,32,12,32]{3,1,2,0:T(8,128)S(1)} fusion(f32[8,12,96,32]{2,3,1,0:T(8,128)S(1)} %fusion.1, s32[32]{0:T(128)S(1)} %compare_select_fusion), kind=kOutput, calls=%fused_computation.18 | convolution fusion | flops 113280000 | bytes 1572992 | tf_op jit(solution)/shard_map/bnyz,yq->bqnz/dot_general | solution.py:54
  116.7 0.9 copy.70
  117.7 1.6 reshape.125
  119.3 3.5 all-to-all-start.3
  128.5 0.7 all-to-all-done.3
  129.3 1.6 reduce.3
  131.5 1.3 fusion.14
  133.1 0.7 broadcast_select_fusion
  133.8 1.0 broadcast_select_fusion.1
  134.8 294.2 %all-reduce.3.cloned.1.call-done = (f32[8,4096]{1,0:T(8,128)}, f32[8,4096]{1,0:T(8,128)}, f32[8,4096]{1,0:T(8,128)}, f32[8,4096]{1,0:T(8,128)}, f32[8,4096]{1,0:...) async-done(((f32[8,4096]{1,0:T(8,128)}, f32[8,4096]{1,0:T(8,128)}, f32[8,4096]{1,0:T(8,128)}, f32[8,4096]{1,0:T(8,128)}, f32[8,4096]{1,0:T(8,128)}, ...) | async-done | bytes 1048592 | tf_op jit(solution)/shard_map/psum | solution.py:15
  429.1 3.6 fusion.43
  432.7 2.7 convolution_add_fusion.6
  435.4 2.7 convolution_add_fusion.5
  438.1 2.7 convolution_add_fusion.4
  440.8 2.9 convolution_add_fusion.3
  443.7 2.7 convolution_add_fusion.2
  446.4 2.7 convolution_add_fusion.1
  449.0 4.4 fusion
  (53 shorter events, 4.4 us)
Async XLA Ops:
  10.5 8.1 %copy-start.3 = (f32[12,9216]{1,0:T(8,128)S(1)}, f32[12,9216]{1,0:T(8,128)}, u32[]{:S(2)}) copy-start(f32[12,9216]{1,0:T(8,128)} %param.7) | copy-start | bytes 1327108
  12.3 13.0 %all-to-all-start = ((f32[8,1,12288]{2,1,0:T(1,128)}), f32[8,1,12288]{2,1,0:T(1,128)S(1)}, u32[]{:S(2)}, u32[]{:S(2)}) async-start(f32[8,1,12288]{2,1,0:T(1,128)} %reshape.119), calls=%async_computation | async-start | bytes 786432 | tf_op jit(solution)/shard_map/all_to_all | solution.py:47
  31.0 7.8 %copy-start = (f32[12,96,96]{2,1,0:T(8,128)S(1)}, f32[12,96,96]{2,1,0:T(8,128)}, u32[]{:S(2)}) copy-start(f32[12,96,96]{2,1,0:T(8,128)} %mul.206) | copy-start | bytes 1327108
  58.7 11.1 %all-to-all-start.1 = ((f32[8,1,12288]{2,1,0:T(1,128)}), f32[8,1,12288]{2,1,0:T(1,128)S(1)}, u32[]{:S(2)}, u32[]{:S(2)}) async-start(f32[8,1,12288]{2,1,0:T(1,128)} %reshape.121), calls=%async_computation.1 | async-start | bytes 786432 | tf_op jit(solution)/shard_map/all_to_all | solution.py:60
  72.0 1.5 copy-start.2
  91.6 8.0 %copy-start.1 = (f32[12,96,96]{2,1,0:T(8,128)S(1)}, f32[12,96,96]{2,1,0:T(8,128)}, u32[]{:S(2)}) copy-start(f32[12,96,96]{2,1,0:T(8,128)} %mul.206) | copy-start | bytes 1327108
  117.7 5.1 %copy-start.13 = (s32[8]{0:T(128)S(1)}, s32[8]{0:T(128)}, u32[]{:S(2)}) copy-start(s32[8]{0:T(128)} %param.11) | copy-start | bytes 100
  119.3 10.0 %all-to-all-start.3 = ((f32[8,1,12288]{2,1,0:T(1,128)}), f32[8,1,12288]{2,1,0:T(1,128)S(1)}, u32[]{:S(2)}, u32[]{:S(2)}) async-start(f32[8,1,12288]{2,1,0:T(1,128)} %reshape.125), calls=%async_computation.3 | async-start | bytes 786432 | tf_op jit(solution)/shard_map/all_to_all | solution.py:60
  122.7 306.3 %all-reduce.3.cloned.1.call-start = ((), (), s32[]{:S(2)}) async-start(), calls=%async_computation.4 | async-start | bytes 2097152 | tf_op jit(solution)/shard_map/psum | solution.py:15
  132.8 296.3 %copy-start.12 = (f32[8,192,8]{1,2,0:T(8,128)S(1)}, f32[8,192,8]{1,2,0:T(8,128)}, u32[]{:S(2)}) copy-start(f32[8,192,8]{1,2,0:T(8,128)} %param.10) | copy-start | bytes 147460
  133.8 298.9 %copy-start.4 = (f32[8,4096]{1,0:T(8,128)}, f32[8,4096]{1,0:T(8,128)S(1)}, u32[]{:S(2)}) copy-start(f32[8,4096]{1,0:T(8,128)S(1)} %get-tuple-element.11) | copy-start | bytes 393220
  429.1 3.6 copy-start.11
  432.7 2.7 copy-start.10
  435.4 2.7 copy-start.9
  438.1 2.7 copy-start.8
  440.8 2.9 copy-start.7
  443.7 2.7 copy-start.6
  446.3 2.7 copy-start.5
Sparse Core Ops, SparseCore 0:
  134.9 294.0 all-reduce.2
where the time goes:
time: 464 us; the launch traced here: 461 us
  waiting for transfers between devices  305 us (66%)
  matrix products  81.9 us (18%)
  between operations  21.2 us (5%)
  local copies, waits for them, and re-layouts  20.1 us (4%)
  starting transfers between devices  14.3 us (3%)
  blocking collectives  9.44 us (2%)
  other arithmetic  8.28 us (2%)
    psum x1, waiting for transfers between devices, spread(): return lax.psum(jnp.where(mine, x, jnp.zeros_like(x)), axis)  294 us
    dot_general x8, matrix products, body(): jnp.dot(rotation[step_index], arrived, precision=lax.Precision.HIGHEST, p...  24.2 us
    dot_general x2, matrix products, to_plane(): jnp.einsum('bnyw,wz->bnyz', real_field, hartley, precision=lax.Precision....  19.6 us
    dot_general x2, matrix products, finish(): jnp.einsum('bnyz,wz->bnyw', along_y, hartley, precision=lax.Precision.HIG...  15.8 us
    dot_general x2, matrix products, to_plane(): jnp.einsum('bnyz,yq->bqnz', along_z, hartley, precision=lax.Precision.HIG...  14.6 us
    all_to_all x1, blocking collectives, to_real(): lax.all_to_all(along_x, 'grid', split_axis=2, concat_axis=1, tiled=True)  9.44 us
  transfers between devices with their start and end apart: 4, of which 4 were waited for; matrix products, arithmetic and copies ran while one was open for 1% of the time, Pallas kernels for 0%

commit v1 on v0

v1 whole, which is shorter than its diff:
```python
import functools

import jax
import jax.numpy as jnp
import ml_dtypes
import numpy as np
from jax import lax
from jax.experimental import pallas as pl
from jax.experimental.pallas import tpu as pltpu
from jax.sharding import PartitionSpec as P

NG = 96
KEEP = 32
SHARDS = 8
BANDS = 8
GROUPS = 32
STEPS = 8
edge_energy = 1.3

F32 = jnp.float32
BF16 = jnp.bfloat16
MESH = pl.DeviceIdType.MESH


def split_table(table):
    hi = table.astype(ml_dtypes.bfloat16)
    lo = (table - hi.astype(np.float64)).astype(ml_dtypes.bfloat16)
    return hi, lo


def hartley_table():
    ordinal = np.arange(KEEP)
    frequency = np.where(ordinal < KEEP // 2, ordinal, ordinal + NG - KEEP)
    angle = (np.arange(NG)[:, None] * frequency[None, :] % NG) * (2.0 * np.pi / NG)
    return (np.cos(angle) + np.sin(angle)) / np.sqrt(float(NG))


def tables():
    hi, lo = split_table(hartley_table())
    zero = np.zeros((), ml_dtypes.bfloat16)
    order = np.array([4 * (r % 24) + r // 24 for r in range(NG)])
    y_syn = np.concatenate([hi, lo, hi, lo], 1)[order]
    block_hi = np.kron(np.eye(4), hi.T.astype(np.float32)).astype(hi.dtype)
    block_lo = np.kron(np.eye(4), lo.T.astype(np.float32)).astype(hi.dtype)
    z_syn = np.concatenate([np.concatenate([block_hi, block_lo], 1)] * 2, 0)
    stacked = np.concatenate([hi, lo, hi, lo], 1)
    x_syn = np.full((SHARDS, 2, 12, 2, 128), zero)
    for half in range(2):
        x_syn[:, half, :, half] = stacked.reshape(SHARDS, 12, 128)
    x_syn = x_syn.reshape(192, 256)
    parts = []
    for t in (hi, lo):
        part = np.full((2, KEEP, SHARDS, 2, 12), zero)
        for half in range(2):
            part[half, :, :, half, :] = t.T.reshape(KEEP, SHARDS, 12)
        parts.append(part.reshape(64, 192))
    x_ana = np.concatenate(parts, 0)
    z_ana = np.concatenate([np.concatenate([block_hi.T, block_lo.T], 1)] * 2, 0)
    y_ana = np.concatenate([np.concatenate([t[order].T] * 2, 1) for t in (hi, lo)], 0)
    signed = np.where(np.arange(KEEP) < KEEP // 2, np.arange(KEEP), np.arange(KEEP) - KEEP)
    square = (signed * signed / float((KEEP // 2) ** 2)).astype(np.float32)
    kinetic = np.float32(edge_energy) * (
        square[:, None, None] + square[None, :, None] + square[None, None, :]
    )
    return y_syn, z_syn, x_syn, x_ana, z_ana, y_ana, kinetic.reshape(KEEP, KEEP * KEEP)


def split(x):
    hi = x.astype(BF16)
    return hi, (x - hi.astype(F32)).astype(BF16)


def dot(a, b):
    return jnp.dot(a, b, preferred_element_type=F32)


def swap_groups(parts):
    lane = lax.broadcasted_iota(jnp.int32, parts[0].shape, 1)
    low = lane < 64
    even = lane % 64 < 32
    half = [None] * 4
    for j in range(2):
        half[j] = jnp.where(low, parts[j], pltpu.roll(parts[j + 2], 64, 1))
        half[j + 2] = jnp.where(low, pltpu.roll(parts[j], 64, 1), parts[j + 2])
    out = []
    for a, b in ((half[0], half[1]), (half[2], half[3])):
        out.append(jnp.where(even, a, pltpu.roll(b, 32, 1)))
        out.append(jnp.where(even, pltpu.roll(a, 96, 1), b))
    return out


def expand_rows(c, tabs, scratch):
    y_syn, z_syn = tabs[:2]
    d1, d2h, d2l, _ = scratch
    ch, cl = split(c)
    along_y = dot(y_syn[...], jnp.concatenate([ch, ch, cl, cl], 0))
    for k8 in range(8):
        cols = slice(128 * k8, 128 * k8 + 128)
        parts = swap_groups([along_y[24 * j : 24 * j + 24, cols] for j in range(4)])
        for m in range(4):
            d1[pl.ds((4 * k8 + m) * 24, 24), :] = parts[m]
    for i in range(6):
        rows = jnp.concatenate([d1[pl.ds(4 * i + j, 32, stride=24), :] for j in range(4)], 0)
        rh, rl = split(rows)
        wide = dot(jnp.concatenate([rh, rl], 1), z_syn[...])
        dh, dl = split(wide[:, :384] + wide[:, 384:])
        d2h[pl.ds(128 * i, 128), :] = dh
        d2l[pl.ds(128 * i, 128), :] = dl


def cross_planes(column, v, tabs, scratch):
    _, _, x_syn, x_ana, _, _ = tabs
    _, d2h, d2l, bz = scratch

    def plane_step(i, carry):
        q = column * 6 + i
        r0 = pl.multiple_of(q * 32, 32)
        r1 = pl.multiple_of(q * 32 + 384, 32)
        h0, l0 = d2h[pl.ds(r0, 32), :], d2l[pl.ds(r0, 32), :]
        h1, l1 = d2h[pl.ds(r1, 32), :], d2l[pl.ds(r1, 32), :]
        field = dot(x_syn[...], jnp.concatenate([h0, h0, l0, l0, h1, h1, l1, l1], 0))
        at = pl.multiple_of(i * 384, 128)
        wh, wl = split(field * v[column, :, :, pl.ds(at, 384)].reshape(192, 384))
        first = dot(x_ana[...], wh)
        back = first[:64] + first[64:] + dot(x_ana[pl.ds(0, 64), :], wl)
        bh, bl = split(back)
        bz[pl.ds(r0, 32), pl.ds(0, 384)] = bh[:32]
        bz[pl.ds(r0, 32), pl.ds(384, 384)] = bl[:32]
        bz[pl.ds(r1, 32), pl.ds(0, 384)] = bh[32:]
        bz[pl.ds(r1, 32), pl.ds(384, 384)] = bl[32:]
        return carry

    lax.fori_loop(0, 6, plane_step, 0, unroll=2)


def contract_rows(tabs, scratch):
    z_ana, y_ana = tabs[4:]
    d1, _, _, bz = scratch
    for i in range(3):
        wide = dot(bz[pl.ds(256 * i, 256), :], z_ana[...])
        d1[pl.ds(256 * i, 256), :] = wide[:, :128] + wide[:, 128:]
    columns = []
    for k8 in range(8):
        parts = [d1[pl.ds(4 * k8 + m, 24, stride=32), :] for m in range(4)]
        columns.append(jnp.concatenate(swap_groups(parts), 0))
    gh, gl = split(jnp.concatenate(columns, 1))
    back = dot(y_ana[...], jnp.concatenate([gh, gl], 0))
    return back[:32] + back[32:]


H_SCRATCH = [
    pltpu.VMEM((768, 128), F32),
    pltpu.VMEM((768, 384), BF16),
    pltpu.VMEM((768, 384), BF16),
    pltpu.VMEM((768, 768), BF16),
]


def filter_kernel(x_ref, v_ref, lower, upper, owners, *refs):
    tabs, kinetic = refs[:6], refs[6]
    filtered, arrived = refs[7:9]
    scratch = refs[9:13]
    (v, pack, coeffs, spread, landed, chunk, gathered, blocks,
     a_send, a_recv, v_send, v_recv, b_send, b_recv, c_send, c_recv, out_sem) = refs[13:]
    band = lax.axis_index("band")
    grid = lax.axis_index("grid")
    z_hi, y, core = band // 8, (band // 2) % 4, band % 2
    z_lo, x = grid // 4, grid % 4
    sibling = (z_hi * 8 + y * 2 + 1 - core, grid)

    def z_step(step):
        z = (z_hi * 2 + z_lo + step) % 8
        return ((z // 2) * 8 + band % 8, (1 - z_lo) * 4 + x)

    def x_step(step):
        return (band, z_lo * 4 + (x + step) % 4)

    def remote(src, dst, send, recv, to):
        return pltpu.make_async_remote_copy(
            src_ref=src, dst_ref=dst, send_sem=send, recv_sem=recv, device_id=to, device_id_type=MESH
        )

    barrier = pltpu.get_barrier_semaphore()

    def greet(to):
        pl.semaphore_signal(barrier, inc=1, device_id=to, device_id_type=MESH)

    @pl.loop(1, SHARDS)
    def _(d):
        greet((band, (grid + d) % SHARDS))

    @pl.loop(1, GROUPS)
    def _(d):
        greet(((band + d) % GROUPS, grid))

    greet(z_step(1))
    greet(z_step(7))

    for r in range(32):
        pack[pl.ds(r, 8, stride=32), :] = x_ref[:, 128 * r : 128 * r + 128]
    for half in range(2):
        for c in range(2):
            at = 4608 * half + 2304 * c
            v[c, grid, pl.ds(12 * half, 12), :] = v_ref[:, at : at + 2304]
    pl.semaphore_wait(barrier, SHARDS - 1 + GROUPS - 1 + 2)

    def exchange(src, dst, first_sem):
        def copy(d, to, block, slot):
            return remote(
                src.at[pl.ds(pl.multiple_of(block * 32, 32), 32), :],
                dst.at[pl.ds(pl.multiple_of(slot * 32, 32), 32), :],
                a_send.at[first_sem + d], a_recv.at[first_sem + d], (band, to),
            )

        def start():
            for d in range(1, SHARDS):
                to = (grid + d) % SHARDS
                copy(d, to, to, grid).start()
            own = pl.ds(pl.multiple_of(grid * 32, 32), 32)
            dst[own, :] = src[own, :]

        def wait():
            for d in range(1, SHARDS):
                came = (grid + SHARDS - d) % SHARDS
                copy(d, came, came, came).wait_recv()

        def wait_sent():
            for d in range(1, SHARDS):
                to = (grid + d) % SHARDS
                copy(d, to, to, grid).wait_send()

        return start, wait, wait_sent

    near = [z_lo * 4 + (x + s) % 4 for s in (0, 3, 1, 2)]
    far = [(1 - z_lo) * 4 + (x + s) % 4 for s in (0, 3, 1, 2)]

    def v_copy(sem, shard, to, piece=None):
        lanes = pl.ds(0, 2304) if piece is None else pl.ds(1152 * piece, 1152)
        ref = v.at[core, shard, :, lanes]
        return remote(ref, ref, v_send.at[sem], v_recv.at[sem], to)

    sent = []

    def v_go(sem, shard, to, piece=None):
        copy = v_copy(sem, shard, to, piece)
        copy.start()
        sent.append(copy)

    def v_come(sem, shard, piece=None):
        v_copy(sem, shard, sibling, piece).wait_recv()

    in_start, in_wait, in_sent = exchange(pack, coeffs, 0)
    in_start()
    v_go(0, near[0], x_step(1))
    v_go(1, near[0], x_step(3))
    for piece, step in ((0, 1), (1, 7)):
        v_go(4 + piece, near[0], z_step(step), piece)
    in_wait()
    c = jnp.concatenate([coeffs[pl.ds(k8, 32, stride=8), :] for k8 in range(8)], 1)
    center = (lower[0] + upper[0]) * 0.5
    inverse = 1.0 / ((upper[0] - lower[0]) * 0.5)
    expand_rows(c, tabs, scratch)

    v_come(0, near[1])
    v_go(2, near[1], x_step(1), 0)
    v_come(1, near[2])
    v_go(3, near[2], x_step(3), 1)
    for s in (1, 2):
        for piece, step in ((0, 1), (1, 7)):
            v_go(4 + 2 * s + piece, near[s], z_step(step), piece)
        v_go(11 + s, near[s], sibling)
    for piece, step in ((0, 1), (1, 7)):
        v_come(2 + piece, near[3], piece)
        v_go(10 + piece, near[3], z_step(step), piece)
        v_go(14 + piece, near[3], sibling, piece)
    for s in range(4):
        for piece in range(2):
            v_come(4 + 2 * s + piece, far[s], piece)
            v_go(16 + 2 * s + piece, far[s], sibling, piece)
    cross_planes(core, v, tabs, scratch)

    def v_twin(sem, shard, piece=None):
        lanes = pl.ds(0, 2304) if piece is None else pl.ds(1152 * piece, 1152)
        ref = v.at[1 - core, shard, :, lanes]
        remote(ref, ref, v_send.at[sem], v_recv.at[sem], sibling).wait_recv()

    v_twin(12, near[1])
    v_twin(13, near[2])
    for piece in range(2):
        v_twin(14 + piece, near[3], piece)
        for s in range(4):
            v_twin(16 + 2 * s + piece, far[s], piece)
    cross_planes(1 - core, v, tabs, scratch)
    shift = kinetic[...] - center
    first = (shift * c + contract_rows(tabs, scratch)) * inverse
    expand_rows(first, tabs, scratch)
    cross_planes(0, v, tabs, scratch)
    cross_planes(1, v, tabs, scratch)
    second = shift * first + contract_rows(tabs, scratch)
    out = (2.0 * inverse) * second - c
    for k8 in range(8):
        spread[pl.ds(k8, 32, stride=8), :] = out[:, 128 * k8 : 128 * k8 + 128]
    out_start, out_wait, out_sent = exchange(spread, landed, SHARDS)
    out_start()
    for copy in sent:
        copy.wait_send()
    in_sent()
    out_wait()
    for r in range(32):
        rows = landed[pl.ds(r, 8, stride=32), :]
        filtered[:, 128 * r : 128 * r + 128] = rows
        chunk[r] = rows

    def b_copy(d, to, block, slot):
        return remote(chunk.at[block], blocks.at[slot], b_send.at[d], b_recv.at[d], (to, grid))

    @pl.loop(1, GROUPS)
    def _(d):
        to = (band + d) % GROUPS
        b_copy(d, to, to, band).start()

    blocks[band] = chunk[band]

    @pl.loop(1, GROUPS)
    def _(d):
        came = (band + GROUPS - d) % GROUPS
        b_copy(d, came, came, came).wait_recv()

    for s in range(STEPS):
        gathered[band, pl.ds(8 * s, 8), :] = blocks[owners[s]]

    def c_copy(sem, index, to):
        ref = gathered.at[index]
        return remote(ref, ref, c_send.at[sem], c_recv.at[sem], (to, grid))

    def index_of(dz, dy, other):
        k = 1 - core if other else core
        return ((z_hi + 4 - dz) % 4) * 8 + ((y + 4 - dy) % 4) * 2 + k

    away = sibling[0]
    for dz in range(1, 4):
        c_copy(dz, band, ((z_hi + dz) % 4) * 8 + band % 8).start()
    for dz in range(4):
        mine = index_of(dz, 0, False)
        if dz:
            c_copy(dz, mine, away).wait_recv()
        for dy in range(1, 4):
            c_copy(4 + 3 * dz + dy - 1, mine, z_hi * 8 + ((y + dy) % 4) * 2 + core).start()
        c_copy(16 + 4 * dz, mine, away).start()
    for dz in range(4):
        for dy in range(1, 4):
            mine = index_of(dz, dy, False)
            c_copy(4 + 3 * dz + dy - 1, mine, away).wait_recv()
            c_copy(16 + 4 * dz + dy, mine, away).start()
    for dz in range(4):
        for dy in range(4):
            c_copy(16 + 4 * dz + dy, index_of(dz, dy, True), away).wait_recv()
    write = pltpu.make_async_copy(gathered, arrived, out_sem)
    write.start()

    @pl.loop(1, GROUPS)
    def _(d):
        to = (band + d) % GROUPS
        b_copy(d, to, to, band).wait_send()

    @pl.loop(1, 32)
    def _(d):
        c_copy(d, band, away).wait_send()

    out_sent()
    write.wait()


VMEM = pl.BlockSpec(memory_space=pltpu.VMEM)
SMEM = pl.BlockSpec(memory_space=pltpu.SMEM)
FILTER = pl.pallas_call(
    filter_kernel,
    out_shape=(
        jax.ShapeDtypeStruct((8, 4096), F32),
        jax.ShapeDtypeStruct((GROUPS, 64, 128), F32),
    ),
    in_specs=[VMEM, VMEM, SMEM, SMEM, SMEM] + [VMEM] * 7,
    out_specs=(VMEM, pl.BlockSpec(memory_space=pl.ANY)),
    scratch_shapes=H_SCRATCH + [
        pltpu.VMEM((2, SHARDS, 24, 2304), F32),
        pltpu.VMEM((256, 128), F32),
        pltpu.VMEM((256, 128), F32),
        pltpu.VMEM((256, 128), F32),
        pltpu.VMEM((256, 128), F32),
        pltpu.VMEM((32, 8, 128), F32),
        pltpu.VMEM((GROUPS, 64, 128), F32),
        pltpu.VMEM((GROUPS, 8, 128), F32),
        pltpu.SemaphoreType.DMA((16,)),
        pltpu.SemaphoreType.DMA((16,)),
        pltpu.SemaphoreType.DMA((24,)),
        pltpu.SemaphoreType.DMA((24,)),
        pltpu.SemaphoreType.DMA((32,)),
        pltpu.SemaphoreType.DMA((32,)),
        pltpu.SemaphoreType.DMA((32,)),
        pltpu.SemaphoreType.DMA((32,)),
        pltpu.SemaphoreType.DMA,
    ],
    compiler_params=pltpu.CompilerParams(
        collective_id=0, has_side_effects=True, vmem_limit_bytes=40 << 20
    ),
    name="filter",
)


def rotate_kernel(rotation, arrived, filtered, filtered_out, residents):
    rh, rl = split(rotation[...])
    left = jnp.concatenate([rh, rl, rh, rl], 1)
    for j in range(4):
        ah, al = split(arrived[j])
        residents[:, 128 * j : 128 * j + 128] = dot(left, jnp.concatenate([ah, ah, al, al], 0))
    filtered_out[...] = filtered[...]


ROTATE = pl.pallas_call(
    rotate_kernel,
    grid=(8,),
    out_shape=(
        jax.ShapeDtypeStruct((8, 4096), F32),
        jax.ShapeDtypeStruct((192, 4096), F32),
    ),
    in_specs=[
        pl.BlockSpec((192, 64), lambda i: (0, 0)),
        pl.BlockSpec((4, 64, 128), lambda i: (i, 0, 0)),
        pl.BlockSpec((8, 512), lambda i: (0, i)),
    ],
    out_specs=(
        pl.BlockSpec((8, 512), lambda i: (0, i)),
        pl.BlockSpec((192, 512), lambda i: (0, i)),
    ),
    name="rotate",
)


def body(block_coeffs, potential, lower_edge, upper_edge, rotation, owners):
    consts = [jnp.asarray(t) for t in tables()]
    filtered, arrived = FILTER(
        block_coeffs, potential, lower_edge, upper_edge, owners, *consts
    )
    coefficients = rotation.transpose(1, 0, 2).reshape(192, 64)
    return tuple(ROTATE(coefficients, arrived, filtered))


def solution(mesh):
    return jax.shard_map(
        body,
        mesh=mesh,
        in_specs=(P("band", "grid"), P("grid", None), P(), P(), P(None, "band", None), P()),
        out_specs=(P("band", "grid"), P("band", "grid")),
        check_vma=False,
    )
```

time: 464 us -> 87.3 us (0.19)
  waiting for transfers between devices: 305 us -> 0 us
  matrix products: 81.9 us -> 0 us
  Pallas kernels: 0 us -> 72.8 us
  between operations: 21.2 us -> 1.95 us
  starting transfers between devices: 14.3 us -> 0 us
  blocking collectives: 9.44 us -> 0 us
  other arithmetic: 8.28 us -> 0 us
  local copies, waits for them, and re-layouts: 20.1 us -> 11.9 us
    psum x1 -> x0, waiting for transfers between devices: 294 us -> none  [spread(): return lax.psum(jnp.where(mine, x, jnp.zeros_like(x)), axis)]
    dot_general x18 -> x0, matrix products: 78.8 us -> none  [the longest x8 24.2 us: body(): jnp.dot(rotation[step_index], arrived, precision=lax.Precision.HIGHEST, p...]
    pallas_call x0 -> x2, Pallas kernels: none -> 72.8 us  [the longest x1 66 us: body(): FILTER(block_coeffs, potential, lower_edge, upper_edge, owners, *consts)]
    all_to_all x3 -> x0, starting transfers between devices: 14.3 us -> none  [the longest x2 7.91 us: to_plane(): lax.all_to_all(along_y, 'grid', split_axis=1, concat_axis=2, tiled=True)]
    all_to_all x3 -> x0, waiting for transfers between devices: 11 us -> none  [the longest x1 5.59 us: to_real(): lax.all_to_all(along_x, 'grid', split_axis=2, concat_axis=1, tiled=True)]
    all_to_all x1 -> x0, blocking collectives: 9.44 us -> none  [to_real(): lax.all_to_all(along_x, 'grid', split_axis=2, concat_axis=1, tiled=True)]
    all_to_all x4 -> x0, other arithmetic: 6.41 us -> none  [the longest x2 3.2 us: to_plane(): lax.all_to_all(along_y, 'grid', split_axis=1, concat_axis=2, tiled=True)]
    transpose x4 -> x0, local copies, waits for them, and re-layouts: 4.66 us -> none  [the longest x2 2.43 us: to_real(): jnp.einsum('bqkz,nk->bqnz', coef_cube, hartley, precision=lax.Precision.H...]
  transfers between devices with their start and end apart: 4 -> 0, of which waited for: 4 -> 0; matrix products, arithmetic and copies ran while one was open for 1% -> 0% of each run, Pallas kernels for 0% -> 0%
where the time goes in v1:
time: 87.3 us; the launch traced here: 86.7 us
  Pallas kernels  72.8 us (83%)
  local copies, waits for them, and re-layouts  11.9 us (14%)
  between operations  1.95 us (2%)
    pallas_call x1, Pallas kernels, body(): FILTER(block_coeffs, potential, lower_edge, upper_edge, owners, *consts)  66 us
    unnamed x24, local copies, waits for them, and re-layouts  10.4 us
    pallas_call x1, Pallas kernels, body(): return tuple(ROTATE(coefficients, arrived, filtered))  6.75 us

profile of v1, /device:TPU:1, one launch (start us, length us, event | category | flops | bytes accessed | tf_op | source)
XLA Modules:
  0.0 86.7 jit_solution(15741064326301768005)
XLA Ops:
  1.9 1.6 %copy.16.rotation = f32[192,64]{1,0:T(8,128)} copy(f32[192,64]{0,1:T(8,128)} %bitcast.3) | data formatting | bytes 98304 | tf_op jit(solution)/shard_map/reshape | solution.py:444
  3.5 0.0 copy-start.1
  3.5 1.1 %copy-done.1 = f32[12,9216]{1,0:T(8,128)S(1)} copy-done((f32[12,9216]{1,0:T(8,128)S(1)}, f32[12,9216]{1,0:T(8,128)}, u32[]{:S(2)}) %copy-start.1) | copy-done | bytes 442392
  4.6 0.0 copy-start.2
  4.6 1.0 %copy-done.2 = bf16[768,256]{1,0:T(8,128)(2,1)S(1)} copy-done((bf16[768,256]{1,0:T(8,128)(2,1)S(1)}, bf16[768,256]{1,0:T(8,128)(2,1)}, u32[]{:S(2)}) %copy-start.2) | copy-done | bytes 393240
  5.6 0.0 copy-start.3
  5.6 1.0 %copy-done.3 = bf16[256,768]{1,0:T(8,128)(2,1)S(1)} copy-done((bf16[256,768]{1,0:T(8,128)(2,1)S(1)}, bf16[256,768]{1,0:T(8,128)(2,1)}, u32[]{:S(2)}) %copy-start.3) | copy-done | bytes 393240
  6.6 0.0 copy-start.4
  6.6 0.9 %copy-done.4 = f32[8,4096]{1,0:T(8,128)S(1)} copy-done((f32[8,4096]{1,0:T(8,128)S(1)}, f32[8,4096]{1,0:T(8,128)}, u32[]{:S(2)}) %copy-start.4) | copy-done | bytes 131096
  7.5 0.0 copy-start.5
  7.5 0.9 %copy-done.5 = f32[32,1024]{1,0:T(8,128)S(1)} copy-done((f32[32,1024]{1,0:T(8,128)S(1)}, f32[32,1024]{1,0:T(8,128)}, u32[]{:S(2)}) %copy-start.5) | copy-done | bytes 131096
  8.4 0.0 copy-start.7
  8.4 0.9 %copy-done.7 = bf16[192,256]{1,0:T(8,128)(2,1)S(1)} copy-done((bf16[192,256]{1,0:T(8,128)(2,1)S(1)}, bf16[192,256]{1,0:T(8,128)(2,1)}, u32[]{:S(2)}) %copy-start.7) | copy-done | bytes 98328
  9.3 0.0 copy-start.8
  9.3 0.8 copy-done.8
  10.1 0.0 copy-start.9
  10.1 0.8 copy-done.9
  10.9 0.0 copy-start.10
  10.9 0.7 copy-done.10
  11.6 0.0 copy-start.11
  11.6 0.7 copy-done.11
  12.3 66.0 %filter.1 = (f32[8,4096]{1,0:T(8,128)S(1)}, f32[32,64,128]{2,1,0:T(8,128)S(1)}) custom-call(f32[8,4096]{1,0:T(8,128)S(1)} %copy-done.4, f32[12,9216]{1,0:T(8,128)S(1)} %copy-done.1, f32[1]{0:T(128)S(6)} %copy.17.lower, f32[1]{0:T(128)S(6)} %copy.18.upper, s32[8]{0:T(128)S(1)} %copy-done.11, bf16[96,128]{1,0:T(8,128)(2,1)S(1)} %copy-done.10, ...), custom_call_target="tpu_custom_call" | custom-call | tf_op jit(solution)/shard_map/filter/pallas_call | solution.py:441
  78.3 0.0 copy-start
  78.3 1.0 %copy-done = f32[32,64,128]{2,1,0:T(8,128)} copy-done((f32[32,64,128]{2,1,0:T(8,128)}, f32[32,64,128]{2,1,0:T(8,128)S(1)}, u32[]{:S(2)}) %copy-start) | copy-done | bytes 1048600
  79.3 0.0 copy-start.6
  79.3 0.6 copy-done.6
  79.9 6.8 %rotate.1 = (f32[8,4096]{1,0:T(8,128)}, f32[192,4096]{1,0:T(8,128)}) custom-call(f32[192,64]{1,0:T(8,128)} %copy.16.rotation, f32[32,64,128]{2,1,0:T(8,128)} %copy-done, f32[8,4096]{1,0:T(8,128)} %copy-done.6), custom_call_target="tpu_custom_call" | custom-call | tf_op jit(solution)/shard_map/rotate/pallas_call | solution.py:445
Async XLA Ops:
  3.5 1.1 %copy-start.1 = (f32[12,9216]{1,0:T(8,128)S(1)}, f32[12,9216]{1,0:T(8,128)}, u32[]{:S(2)}) copy-start(f32[12,9216]{1,0:T(8,128)} %v_ref.1) | copy-start | bytes 1327108
  4.6 1.0 %copy-start.2 = (bf16[768,256]{1,0:T(8,128)(2,1)S(1)}, bf16[768,256]{1,0:T(8,128)(2,1)}, u32[]{:S(2)}) copy-start(bf16[768,256]{1,0:T(8,128)(2,1)} %constant.18.clone.refs_4_) | copy-start | bytes 1179652
  5.6 1.0 %copy-start.3 = (bf16[256,768]{1,0:T(8,128)(2,1)S(1)}, bf16[256,768]{1,0:T(8,128)(2,1)}, u32[]{:S(2)}) copy-start(bf16[256,768]{1,0:T(8,128)(2,1)} %constant.15.clone.refs_1_) | copy-start | bytes 1179652
  6.6 0.9 %copy-start.4 = (f32[8,4096]{1,0:T(8,128)S(1)}, f32[8,4096]{1,0:T(8,128)}, u32[]{:S(2)}) copy-start(f32[8,4096]{1,0:T(8,128)} %x_ref.1) | copy-start | bytes 393220
  7.5 0.9 %copy-start.5 = (f32[32,1024]{1,0:T(8,128)S(1)}, f32[32,1024]{1,0:T(8,128)}, u32[]{:S(2)}) copy-start(f32[32,1024]{1,0:T(8,128)} %constant.20.clone.refs_6_) | copy-start | bytes 393220
  8.4 0.9 %copy-start.7 = (bf16[192,256]{1,0:T(8,128)(2,1)S(1)}, bf16[192,256]{1,0:T(8,128)(2,1)}, u32[]{:S(2)}) copy-start(bf16[192,256]{1,0:T(8,128)(2,1)} %constant.16.clone.refs_2_) | copy-start | bytes 294916
  9.3 0.8 copy-start.8
  10.1 0.8 copy-start.9
  10.9 0.7 copy-start.10
  11.6 0.7 copy-start.11
  78.3 1.0 %copy-start = (f32[32,64,128]{2,1,0:T(8,128)}, f32[32,64,128]{2,1,0:T(8,128)S(1)}, u32[]{:S(2)}) copy-start(f32[32,64,128]{2,1,0:T(8,128)S(1)} %get-tuple-element.4.arrived) | copy-start | bytes 3145732
  79.3 0.6 copy-start.6

commit v2 on v1

v2 whole, which is shorter than its diff:
```python
import functools

import jax
import jax.numpy as jnp
import ml_dtypes
import numpy as np
from jax import lax
from jax.experimental import pallas as pl
from jax.experimental.pallas import tpu as pltpu
from jax.sharding import PartitionSpec as P

NG = 96
KEEP = 32
NS = 64
SHARDS = 8
BANDS = 8
GROUPS = 32
STEPS = 8
edge_energy = 1.3

F32 = jnp.float32
BF16 = jnp.bfloat16
MESH = pl.DeviceIdType.MESH
VMEM_LIMIT = 58 << 20


def split_table(table):
    hi = table.astype(ml_dtypes.bfloat16)
    lo = (table - hi.astype(np.float64)).astype(ml_dtypes.bfloat16)
    return hi, lo


def hartley_table():
    ordinal = np.arange(KEEP)
    frequency = np.where(ordinal < KEEP // 2, ordinal, ordinal + NG - KEEP)
    angle = (np.arange(NG)[:, None] * frequency[None, :] % NG) * (2.0 * np.pi / NG)
    return (np.cos(angle) + np.sin(angle)) / np.sqrt(float(NG))


def fine_points():
    return np.arange(NG) * (2.0 * np.pi / NG)


def short_points():
    return (np.arange(NS) + 0.5) * (2.0 * np.pi / NS)


def short_table():
    ordinal = np.arange(KEEP)
    signed = np.where(ordinal < KEEP // 2, ordinal, ordinal - KEEP)
    angle = short_points()[:, None] * signed[None, :]
    return (np.cos(angle) + np.sin(angle)) / np.sqrt(float(NG))


def resample_table():
    gap = short_points()[:, None] - fine_points()[None, :]
    table = 1.0 + 2.0 * sum(np.cos(f * gap) for f in range(1, KEEP))
    table = table + np.sin(KEEP * short_points())[:, None] * np.sin(KEEP * fine_points())[None, :]
    return table / NS


def four_blocks(table):
    return np.kron(np.eye(4), table.astype(np.float32)).astype(table.dtype)


def tables():
    hi, lo = split_table(hartley_table())
    short_hi, short_lo = split_table(short_table())
    fit_hi, fit_lo = split_table(resample_table())
    zero = np.zeros((), ml_dtypes.bfloat16)
    order = np.array([4 * (r % 16) + r // 16 for r in range(NS)])
    y_syn = np.concatenate([short_hi, short_lo, short_hi, short_lo], 1)[order]
    z_syn = np.concatenate([four_blocks(short_hi.T), four_blocks(short_lo.T)], 1)
    stacked = np.concatenate([hi, lo, hi, lo], 1)
    x_syn = np.full((SHARDS, 2, 12, 2, 128), zero)
    for half in range(2):
        x_syn[:, half, :, half] = stacked.reshape(SHARDS, 12, 128)
    x_syn = x_syn.reshape(192, 256)
    parts = []
    for t in (hi, lo):
        part = np.full((2, KEEP, SHARDS, 2, 12), zero)
        for half in range(2):
            part[half, :, :, half, :] = t.T.reshape(KEEP, SHARDS, 12)
        parts.append(part.reshape(64, 192))
    x_ana = np.concatenate(parts, 0)
    z_ana = np.concatenate([four_blocks(short_hi), four_blocks(short_lo)], 1)
    y_ana = np.concatenate([np.concatenate([t[order].T] * 2, 1) for t in (short_hi, short_lo)], 0)
    z_fit = np.concatenate([four_blocks(fit_hi.T), four_blocks(fit_lo.T)], 1)
    rows = np.array([2 * (r % 32) + r // 32 for r in range(NS)])
    columns = np.array([4 * (r % 24) + r // 24 for r in range(NG)])
    y_fit = np.concatenate([t[rows][:, columns] for t in (fit_hi, fit_lo, fit_hi, fit_lo)], 1)
    return y_syn, z_syn, x_syn, x_ana, z_ana, y_ana, z_fit, y_fit


def kinetic_plane():
    def square(k):
        signed = jnp.where(k < KEEP // 2, k, k - KEEP)
        return (signed * signed).astype(F32) * (1.0 / (KEEP // 2) ** 2)

    ky = lax.broadcasted_iota(jnp.int32, (KEEP, KEEP * KEEP), 0)
    lane = lax.broadcasted_iota(jnp.int32, (KEEP, KEEP * KEEP), 1)
    return edge_energy * (square(ky) + square(lane // KEEP) + square(lane % KEEP))


def split(x):
    hi = x.astype(BF16)
    return hi, (x - hi.astype(F32)).astype(BF16)


def dot(a, b):
    return jnp.dot(a, b, preferred_element_type=F32)


def swap_groups(parts):
    lane = lax.broadcasted_iota(jnp.int32, parts[0].shape, 1)
    low = lane < 64
    even = lane % 64 < 32
    half = [None] * 4
    for j in range(2):
        half[j] = jnp.where(low, parts[j], pltpu.roll(parts[j + 2], 64, 1))
        half[j + 2] = jnp.where(low, pltpu.roll(parts[j], 64, 1), parts[j + 2])
    out = []
    for a, b in ((half[0], half[1]), (half[2], half[3])):
        out.append(jnp.where(even, a, pltpu.roll(b, 32, 1)))
        out.append(jnp.where(even, pltpu.roll(a, 96, 1), b))
    return out


def twofold(a, table, width):
    ah, al = split(a)
    wide = dot(ah, table[...])
    return wide[:, :width] + wide[:, width:] + dot(al, table[:, :width])


def fit_potential(v_ref, tabs, planes, own):
    z_fit, y_fit = tabs[6:]
    lane = lax.broadcasted_iota(jnp.int32, (32, 128), 1)
    low = lane < 64
    blank = jnp.zeros((4, 384), F32)
    for i in range(4):
        blocks = []
        for c in range(6 * i, 6 * i + 6):
            blocks += [v_ref[:, 384 * c : 384 * c + 384], blank]
        rows = jnp.concatenate(blocks, 0)
        fit = twofold(rows, z_fit, 256)
        for tile in range(2):
            planes[tile, pl.ds(96 * i, 96), :] = fit[:, 128 * tile : 128 * tile + 128]
    columns = []
    for n in range(0, 12, 2):
        parts = []
        for j in range(4):
            a = planes[j // 2, pl.ds(n, 24, stride=16), :]
            b = planes[j // 2, pl.ds(n + 1, 24, stride=16), :]
            if j % 2 == 0:
                parts.append(jnp.where(low[:24], a, pltpu.roll(b, 64, 1)))
            else:
                parts.append(jnp.where(low[:24], pltpu.roll(a, 64, 1), b))
        columns.append(jnp.concatenate(parts, 0))
    hi, lo = split(jnp.concatenate(columns, 1))
    fit = dot(y_fit[...], jnp.concatenate([hi, hi, lo, lo], 0))
    for n in range(0, 12, 2):
        even, odd = fit[:32, 64 * n : 64 * n + 128], fit[32:, 64 * n : 64 * n + 128]
        first = jnp.where(low, even, pltpu.roll(odd, 64, 1))
        second = jnp.where(low, pltpu.roll(even, 64, 1), odd)
        for p, plane in ((n, first), (n + 1, second)):
            for half in range(2):
                for column in range(2):
                    t = 16 * half + 8 * column
                    own[pl.ds(192 * column + 12 * half + p, 8, stride=24), :] = plane[t : t + 8]


def expand_rows(c, tabs, scratch):
    y_syn, z_syn = tabs[:2]
    d1, d2h, d2l, _ = scratch
    ch, cl = split(c)
    along_y = dot(y_syn[...], jnp.concatenate([ch, ch, cl, cl], 0))
    for k8 in range(8):
        cols = slice(128 * k8, 128 * k8 + 128)
        parts = swap_groups([along_y[16 * j : 16 * j + 16, cols] for j in range(4)])
        for m in range(4):
            d1[pl.ds((4 * k8 + m) * 16, 16), :] = parts[m]
    for i in range(2):
        rows = jnp.concatenate([d1[pl.ds(8 * i + j, 32, stride=16), :] for j in range(8)], 0)
        dh, dl = split(twofold(rows, z_syn, 256))
        d2h[pl.ds(256 * i, 256), :] = dh
        d2l[pl.ds(256 * i, 256), :] = dl


def cross_planes(column, v, tabs, scratch):
    _, _, x_syn, x_ana = tabs[:4]
    _, d2h, d2l, bz = scratch

    def plane_step(i, carry):
        q = column * 4 + i
        r0 = pl.multiple_of(q * 32, 32)
        r1 = pl.multiple_of(q * 32 + 256, 32)
        h0, l0 = d2h[pl.ds(r0, 32), :], d2l[pl.ds(r0, 32), :]
        h1, l1 = d2h[pl.ds(r1, 32), :], d2l[pl.ds(r1, 32), :]
        field = dot(x_syn[...], jnp.concatenate([h0, h0, l0, l0, h1, h1, l1, l1], 0))
        tiles = [
            v[column, :, pl.ds(pl.multiple_of(48 * i + 24 * j, 8), 24), :].reshape(192, 128)
            for j in range(2)
        ]
        wh, wl = split(field * jnp.concatenate(tiles, 1))
        first = dot(x_ana[...], wh)
        back = first[:64] + first[64:] + dot(x_ana[pl.ds(0, 64), :], wl)
        bz[pl.ds(r0, 32), :] = back[:32]
        bz[pl.ds(r1, 32), :] = back[32:]
        return carry

    lax.fori_loop(0, 4, plane_step, 0, unroll=True)


def contract_rows(tabs, scratch):
    z_ana, y_ana = tabs[4:6]
    d1, _, _, bz = scratch
    for i in range(2):
        d1[pl.ds(256 * i, 256), :] = twofold(bz[pl.ds(256 * i, 256), :], z_ana, 128)
    columns = []
    for k8 in range(8):
        parts = [d1[pl.ds(4 * k8 + m, 16, stride=32), :] for m in range(4)]
        columns.append(jnp.concatenate(swap_groups(parts), 0))
    gh, gl = split(jnp.concatenate(columns, 1))
    back = dot(y_ana[...], jnp.concatenate([gh, gl], 0))
    return back[:32] + back[32:]


H_SCRATCH = [
    pltpu.VMEM((512, 128), F32),
    pltpu.VMEM((512, 256), BF16),
    pltpu.VMEM((512, 256), BF16),
    pltpu.VMEM((512, 256), F32),
]


def filter_kernel(x_hbm, v_hbm, rotation_hbm, lower, upper, owners, *refs):
    tables_hbm = refs[:8]
    filtered, residents = refs[8:10]
    x_ref, v_ref, rotation_ref = refs[10:13]
    tabs = refs[13:21]
    scratch = refs[21:25]
    (v, planes, own, pack, coeffs, spread, landed, chunk, gathered, blocks, left, rotated, local_sem,
     a_send, a_recv, v_send, v_recv, b_send, b_recv, c_send, c_recv, out_sem) = refs[25:]
    band = lax.axis_index("band")
    grid = lax.axis_index("grid")
    z_hi, y, core = band // 8, (band // 2) % 4, band % 2
    z_lo, x = grid // 4, grid % 4
    sibling = (z_hi * 8 + y * 2 + 1 - core, grid)

    def z_step(step):
        z = (z_hi * 2 + z_lo + step) % 8
        return ((z // 2) * 8 + band % 8, (1 - z_lo) * 4 + x)

    def x_step(step):
        return (band, z_lo * 4 + (x + step) % 4)

    def y_step(step):
        return (z_hi * 8 + ((y + step) % 4) * 2 + core, grid)

    def remote(src, dst, send, recv, to):
        return pltpu.make_async_remote_copy(
            src_ref=src, dst_ref=dst, send_sem=send, recv_sem=recv, device_id=to, device_id_type=MESH
        )

    sources = (x_hbm, v_hbm, tables_hbm[6], tables_hbm[7], rotation_hbm) + tuple(tables_hbm[:6])
    targets = (x_ref, v_ref, tabs[6], tabs[7], rotation_ref) + tuple(tabs[:6])
    fetches = [
        pltpu.make_async_copy(src, dst, local_sem.at[i])
        for i, (src, dst) in enumerate(zip(sources, targets))
    ]
    for fetch in fetches:
        fetch.start()

    barrier = pltpu.get_barrier_semaphore()

    def greet(to):
        pl.semaphore_signal(barrier, inc=1, device_id=to, device_id_type=MESH)

    @pl.loop(1, SHARDS)
    def _(d):
        greet((band, (grid + d) % SHARDS))

    @pl.loop(1, GROUPS)
    def _(d):
        greet(((band + d) % GROUPS, grid))

    greet(z_step(1))
    greet(z_step(7))

    fetches[0].wait()
    for r in range(32):
        pack[pl.ds(r, 8, stride=32), :] = x_ref[:, 128 * r : 128 * r + 128]
    pl.semaphore_wait(barrier, SHARDS - 1 + GROUPS - 1 + 2)

    def exchange(src, dst, first_sem):
        def copy(d, to, block, slot):
            return remote(
                src.at[pl.ds(pl.multiple_of(block * 32, 32), 32), :],
                dst.at[pl.ds(pl.multiple_of(slot * 32, 32), 32), :],
                a_send.at[first_sem + d], a_recv.at[first_sem + d], (band, to),
            )

        def start():
            for d in range(1, SHARDS):
                to = (grid + d) % SHARDS
                copy(d, to, to, grid).start()
            own = pl.ds(pl.multiple_of(grid * 32, 32), 32)
            dst[own, :] = src[own, :]

        def wait():
            for d in range(1, SHARDS):
                came = (grid + SHARDS - d) % SHARDS
                copy(d, came, came, came).wait_recv()

        def wait_sent():
            for d in range(1, SHARDS):
                to = (grid + d) % SHARDS
                copy(d, to, to, grid).wait_send()

        return start, wait, wait_sent

    near = [z_lo * 4 + (x + s) % 4 for s in (0, 3, 1, 2)]
    far = [(1 - z_lo) * 4 + (x + s) % 4 for s in (0, 3, 1, 2)]

    def v_copy(sem, shard, to, part=None, column=core):
        rows = pl.ds(0, 192) if part is None else pl.ds(96 * part, 96)
        ref = v.at[column, shard, rows, :]
        return remote(ref, ref, v_send.at[sem], v_recv.at[sem], to)

    sent = []

    def v_go(*where):
        copy = v_copy(*where)
        copy.start()
        sent.append(copy)

    def along_z(s):
        for part, step in ((0, 1), (1, 7)):
            v_go(3 + 2 * s + part, near[s], z_step(step), part)

    def from_x(s):
        v_copy(s - 1, near[s], sibling).wait_recv()
        along_z(s)
        v_go(10 + s, near[s], sibling)

    def from_z(s):
        for part in range(2):
            v_copy(3 + 2 * s + part, far[s], sibling, part).wait_recv()
        v_go(14 + s, far[s], sibling)

    in_start, in_wait, in_sent = exchange(pack, coeffs, 0)
    in_start()
    for fetch in fetches[1:4]:
        fetch.wait()
    fit_potential(v_ref, tabs, planes, own)
    for column in range(2):
        v[column, grid] = own[192 * column : 192 * column + 192]
    for s, step in ((1, 1), (2, 3), (3, 2)):
        v_go(s - 1, near[0], x_step(step))
    along_z(0)
    for fetch in fetches[4:]:
        fetch.wait()
    rh, rl = split(rotation_ref[...].T)
    left[...] = jnp.concatenate([rh, rl, rh, rl], 1)
    center = (lower[0] + upper[0]) * 0.5
    inverse = 1.0 / ((upper[0] - lower[0]) * 0.5)
    in_wait()
    c = jnp.concatenate([coeffs[pl.ds(k8, 32, stride=8), :] for k8 in range(8)], 1)
    expand_rows(c, tabs, scratch)
    from_z(0)
    for s in range(1, 4):
        from_x(s)
    for s in range(1, 4):
        from_z(s)
    cross_planes(core, v, tabs, scratch)
    for s in range(1, 4):
        v_copy(10 + s, near[s], sibling, None, 1 - core).wait_recv()
    for s in range(4):
        v_copy(14 + s, far[s], sibling, None, 1 - core).wait_recv()
    cross_planes(1 - core, v, tabs, scratch)
    shift = kinetic_plane() - center
    first = (shift * c + contract_rows(tabs, scratch)) * inverse
    expand_rows(first, tabs, scratch)
    cross_planes(0, v, tabs, scratch)
    cross_planes(1, v, tabs, scratch)
    second = shift * first + contract_rows(tabs, scratch)
    out = (2.0 * inverse) * second - c
    for k8 in range(8):
        spread[pl.ds(k8, 32, stride=8), :] = out[:, 128 * k8 : 128 * k8 + 128]
    out_start, out_wait, out_sent = exchange(spread, landed, SHARDS)
    out_start()
    for copy in sent:
        copy.wait_send()
    in_sent()
    out_wait()
    for r in range(32):
        rows = landed[pl.ds(r, 8, stride=32), :]
        x_ref[:, 128 * r : 128 * r + 128] = rows
        chunk[r] = rows

    def b_copy(d, to, block, slot):
        return remote(chunk.at[block], blocks.at[slot], b_send.at[d], b_recv.at[d], (to, grid))

    @pl.loop(1, GROUPS)
    def _(d):
        to = (band + d) % GROUPS
        b_copy(d, to, to, band).start()

    write = pltpu.make_async_copy(x_ref, filtered, local_sem.at[0])
    write.start()
    blocks[band] = chunk[band]

    @pl.loop(1, GROUPS)
    def _(d):
        came = (band + GROUPS - d) % GROUPS
        b_copy(d, came, came, came).wait_recv()

    for s in range(STEPS):
        gathered[band, pl.ds(8 * s, 8), :] = blocks[owners[s]]

    def c_copy(sem, index, to):
        ref = gathered.at[index]
        return remote(ref, ref, c_send.at[sem], c_recv.at[sem], (to, grid))

    def index_of(dz, dy, other):
        k = 1 - core if other else core
        return ((z_hi + 4 - dz) % 4) * 8 + ((y + 4 - dy) % 4) * 2 + k

    away = sibling[0]
    for dz in range(1, 4):
        c_copy(dz, band, ((z_hi + dz) % 4) * 8 + band % 8).start()
    for dz in range(4):
        mine = index_of(dz, 0, False)
        if dz:
            c_copy(dz, mine, away).wait_recv()
        for dy in range(1, 4):
            c_copy(4 + 3 * dz + dy - 1, mine, z_hi * 8 + ((y + dy) % 4) * 2 + core).start()
        c_copy(16 + 4 * dz, mine, away).start()
    for dz in range(4):
        for dy in range(1, 4):
            mine = index_of(dz, dy, False)
            c_copy(4 + 3 * dz + dy - 1, mine, away).wait_recv()
            c_copy(16 + 4 * dz + dy, mine, away).start()

    writes = []
    for dz in range(4):
        for dy in range(4):
            c_copy(16 + 4 * dz + dy, index_of(dz, dy, True), away).wait_recv()
            pair = ((z_hi + 4 - dz) % 4) * 4 + (y + 4 - dy) % 4
            ah, al = split(jnp.concatenate([gathered[2 * pair], gathered[2 * pair + 1]], 1))
            at = pl.ds(pl.multiple_of(pair * 256, 256), 256)
            rotated[:, at] = dot(left[...], jnp.concatenate([ah, ah, al, al], 0))
            writes.append(pltpu.make_async_copy(rotated.at[:, at], residents.at[:, at], out_sem.at[4 * dz + dy]))
            writes[-1].start()

    @pl.loop(1, GROUPS)
    def _(d):
        to = (band + d) % GROUPS
        b_copy(d, to, to, band).wait_send()

    @pl.loop(1, 32)
    def _(d):
        c_copy(d, band, away).wait_send()

    out_sent()
    write.wait()
    for copy in writes:
        copy.wait()


SMEM = pl.BlockSpec(memory_space=pltpu.SMEM)
ANY = pl.BlockSpec(memory_space=pl.ANY)
FILTER = pl.pallas_call(
    filter_kernel,
    out_shape=(
        jax.ShapeDtypeStruct((8, 4096), F32),
        jax.ShapeDtypeStruct((192, 4096), F32),
    ),
    in_specs=[ANY] * 3 + [SMEM] * 3 + [ANY] * 8,
    out_specs=(ANY, ANY),
    scratch_shapes=[
        pltpu.VMEM((8, 4096), F32),
        pltpu.VMEM((12, 9216), F32),
        pltpu.VMEM((64, 192), F32),
        pltpu.VMEM((64, 128), BF16),
        pltpu.VMEM((128, 512), BF16),
        pltpu.VMEM((192, 256), BF16),
        pltpu.VMEM((128, 192), BF16),
        pltpu.VMEM((256, 256), BF16),
        pltpu.VMEM((64, 128), BF16),
        pltpu.VMEM((384, 512), BF16),
        pltpu.VMEM((64, 384), BF16),
    ] + H_SCRATCH + [
        pltpu.VMEM((2, SHARDS, 192, 128), F32),
        pltpu.VMEM((2, 384, 128), F32),
        pltpu.VMEM((384, 128), F32),
        pltpu.VMEM((256, 128), F32),
        pltpu.VMEM((256, 128), F32),
        pltpu.VMEM((256, 128), F32),
        pltpu.VMEM((256, 128), F32),
        pltpu.VMEM((32, 8, 128), F32),
        pltpu.VMEM((GROUPS, 64, 128), F32),
        pltpu.VMEM((GROUPS, 8, 128), F32),
        pltpu.VMEM((192, 256), BF16),
        pltpu.VMEM((192, 4096), F32),
        pltpu.SemaphoreType.DMA((11,)),
        pltpu.SemaphoreType.DMA((16,)),
        pltpu.SemaphoreType.DMA((16,)),
        pltpu.SemaphoreType.DMA((18,)),
        pltpu.SemaphoreType.DMA((18,)),
        pltpu.SemaphoreType.DMA((32,)),
        pltpu.SemaphoreType.DMA((32,)),
        pltpu.SemaphoreType.DMA((32,)),
        pltpu.SemaphoreType.DMA((32,)),
        pltpu.SemaphoreType.DMA((16,)),
    ],
    compiler_params=pltpu.CompilerParams(
        collective_id=0, has_side_effects=True, vmem_limit_bytes=VMEM_LIMIT
    ),
    name="filter",
)


def body(block_coeffs, potential, lower_edge, upper_edge, rotation, owners):
    consts = [jnp.asarray(t) for t in tables()]
    coefficients = rotation.transpose(0, 2, 1).reshape(64, 192)
    return tuple(
        FILTER(block_coeffs, potential, coefficients, lower_edge, upper_edge, owners, *consts)
    )


def solution(mesh):
    return jax.shard_map(
        body,
        mesh=mesh,
        in_specs=(P("band", "grid"), P("grid", None), P(), P(), P(None, "band", None), P()),
        out_specs=(P("band", "grid"), P("band", "grid")),
        check_vma=False,
    )
```

time: 87.3 us -> 64.1 us (0.73)
  Pallas kernels: 72.8 us -> 56.2 us
  local copies, waits for them, and re-layouts: 11.9 us -> 5.42 us
    pallas_call x2 -> x1, Pallas kernels: 72.8 us -> 56.2 us  [body(): FILTER(block_coeffs, potential, coefficients, lower_edge, upper_edge, own...]
    unnamed x24 -> x2, local copies, waits for them, and re-layouts: 10.4 us -> 5.42 us
    reshape x1 -> x0, local copies, waits for them, and re-layouts: 1.59 us -> none  [body(): coefficients = rotation.transpose(1, 0, 2).reshape(192, 64)]
where the time goes in v2:
time: 64.1 us; the launch traced here: 63.6 us
  Pallas kernels  56.2 us (88%)
  local copies, waits for them, and re-layouts  5.42 us (8%)
  between operations  1.93 us (3%)
    pallas_call x1, Pallas kernels, body(): FILTER(block_coeffs, potential, coefficients, lower_edge, upper_edge, own...  56.2 us
    unnamed x2, local copies, waits for them, and re-layouts  5.42 us

profile of v2, /device:TPU:1, one launch (start us, length us, event | category | flops | bytes accessed | tf_op | source)
XLA Modules:
  0.0 63.6 jit_solution(16177115578602918862)
XLA Ops:
  1.9 56.2 %filter.1 = (f32[8,4096]{1,0:T(8,128)}, f32[192,4096]{1,0:T(8,128)}) custom-call(f32[8,4096]{1,0:T(8,128)} %x_hbm.1, f32[12,9216]{1,0:T(8,128)} %v_hbm.1, f32[64,192]{1,0:T(8,128)} %bitcast.3, f32[1]{0:T(128)S(6)} %copy.18.lower, f32[1]{0:T(128)S(6)} %copy.19.upper, s32[8]{0:T(128)} %owners.1, bf16[64,128]{1,0:T(8,128)(2,1)} %constant.16.clone.refs_0_, ...), custom_call_target="tpu_custom_call" | custom-call | tf_op jit(solution)/shard_map/filter/pallas_call | solution.py:528
  58.1 1.6 %copy.20 = f32[8,4096]{1,0:T(8,128)} copy(f32[8,4096]{1,0:T(8,128)} %get-tuple-element.4) | data formatting | bytes 262144
  59.7 3.9 %copy.21 = f32[192,4096]{1,0:T(8,128)} copy(f32[192,4096]{1,0:T(8,128)} %get-tuple-element.5) | data formatting | bytes 6291456

commit v3 on v2

--- a/solution.py
+++ b/solution.py
@@ -15,6 +15,7 @@
 SHARDS = 8
 BANDS = 8
 GROUPS = 32
+CHIPS = 16
 STEPS = 8
 edge_energy = 1.3
 
@@ -233,17 +234,17 @@
 ]
 
 
-def filter_kernel(x_hbm, v_hbm, rotation_hbm, lower, upper, owners, *refs):
+def filter_kernel(x_hbm, v_hbm, lower, upper, owners, *refs):
     tables_hbm = refs[:8]
-    filtered, residents = refs[8:10]
-    x_ref, v_ref, rotation_ref = refs[10:13]
-    tabs = refs[13:21]
-    scratch = refs[21:25]
-    (v, planes, own, pack, coeffs, spread, landed, chunk, gathered, blocks, left, rotated, local_sem,
-     a_send, a_recv, v_send, v_recv, b_send, b_recv, c_send, c_recv, out_sem) = refs[25:]
+    filtered, arrived = refs[8:10]
+    x_ref, v_ref = refs[10:12]
+    tabs = refs[12:20]
+    scratch = refs[20:24]
+    (v, planes, own, pack, coeffs, spread, landed, chunk, pairs, gathered, blocks, local_sem,
+     a_send, a_recv, v_send, v_recv, b_send, b_recv, c_send, c_recv) = refs[24:]
     band = lax.axis_index("band")
     grid = lax.axis_index("grid")
-    z_hi, y, core = band // 8, (band // 2) % 4, band % 2
+    z_hi, y, core, chip = band // 8, (band // 2) % 4, band % 2, band // 2
     z_lo, x = grid // 4, grid % 4
     sibling = (z_hi * 8 + y * 2 + 1 - core, grid)
 
@@ -262,8 +263,8 @@
             src_ref=src, dst_ref=dst, send_sem=send, recv_sem=recv, device_id=to, device_id_type=MESH
         )
 
-    sources = (x_hbm, v_hbm, tables_hbm[6], tables_hbm[7], rotation_hbm) + tuple(tables_hbm[:6])
-    targets = (x_ref, v_ref, tabs[6], tabs[7], rotation_ref) + tuple(tabs[:6])
+    sources = (v_hbm, tables_hbm[6], tables_hbm[7], x_hbm) + tuple(tables_hbm[:6])
+    targets = (v_ref, tabs[6], tabs[7], x_ref) + tuple(tabs[:6])
     fetches = [
         pltpu.make_async_copy(src, dst, local_sem.at[i])
         for i, (src, dst) in enumerate(zip(sources, targets))
@@ -280,44 +281,40 @@
     def _(d):
         greet((band, (grid + d) % SHARDS))
 
-    @pl.loop(1, GROUPS)
+    @pl.loop(1, CHIPS)
     def _(d):
-        greet(((band + d) % GROUPS, grid))
-
+        greet((((chip + d) % CHIPS) * 2 + core, grid))
+
+    greet(sibling)
     greet(z_step(1))
     greet(z_step(7))
 
-    fetches[0].wait()
-    for r in range(32):
-        pack[pl.ds(r, 8, stride=32), :] = x_ref[:, 128 * r : 128 * r + 128]
-    pl.semaphore_wait(barrier, SHARDS - 1 + GROUPS - 1 + 2)
-
-    def exchange(src, dst, first_sem):
-        def copy(d, to, block, slot):
+    for fetch in fetches[:3]:
+        fetch.wait()
+    fit_potential(v_ref, tabs, planes, own)
+    for column in range(2):
+        v[column, grid] = own[192 * column : 192 * column + 192]
+    pl.semaphore_wait(barrier, SHARDS - 1 + CHIPS - 1 + 3)
+
+    def exchange(src, dst, sem):
+        def copy(to, block, slot, rows=32):
             return remote(
-                src.at[pl.ds(pl.multiple_of(block * 32, 32), 32), :],
-                dst.at[pl.ds(pl.multiple_of(slot * 32, 32), 32), :],
-                a_send.at[first_sem + d], a_recv.at[first_sem + d], (band, to),
+                src.at[pl.ds(pl.multiple_of(block * 32, 32), rows), :],
+                dst.at[pl.ds(pl.multiple_of(slot * 32, 32), rows), :],
+                a_send.at[sem], a_recv.at[sem], (band, to),
             )
 
         def start():
-            for d in range(1, SHARDS):
-                to = (grid + d) % SHARDS
-                copy(d, to, to, grid).start()
+            for dz, dx in ((1, 2), (1, 1), (1, 3), (0, 2), (1, 0), (0, 1), (0, 3)):
+                to = (z_lo + dz) % 2 * 4 + (x + dx) % 4
+                copy(to, to, grid).start()
             own = pl.ds(pl.multiple_of(grid * 32, 32), 32)
             dst[own, :] = src[own, :]
 
-        def wait():
-            for d in range(1, SHARDS):
-                came = (grid + SHARDS - d) % SHARDS
-                copy(d, came, came, came).wait_recv()
-
-        def wait_sent():
-            for d in range(1, SHARDS):
-                to = (grid + d) % SHARDS
-                copy(d, to, to, grid).wait_send()
-
-        return start, wait, wait_sent
+        def all_of_them():
+            return copy((grid + 1) % SHARDS, 0, 0, 32 * (SHARDS - 1))
+
+        return start, all_of_them().wait_recv, all_of_them().wait_send
 
     near = [z_lo * 4 + (x + s) % 4 for s in (0, 3, 1, 2)]
     far = [(1 - z_lo) * 4 + (x + s) % 4 for s in (0, 3, 1, 2)]
@@ -334,49 +331,55 @@
         copy.start()
         sent.append(copy)
 
-    def along_z(s):
-        for part, step in ((0, 1), (1, 7)):
-            v_go(3 + 2 * s + part, near[s], z_step(step), part)
-
-    def from_x(s):
-        v_copy(s - 1, near[s], sibling).wait_recv()
-        along_z(s)
-        v_go(10 + s, near[s], sibling)
+    def along_z(s, part):
+        v_go(6 + 2 * s + part, near[s], z_step(7 if part else 1), part)
+
+    def from_x(sem, s, part):
+        v_copy(sem, near[s], sibling, part).wait_recv()
+        along_z(s, part)
 
     def from_z(s):
         for part in range(2):
-            v_copy(3 + 2 * s + part, far[s], sibling, part).wait_recv()
-        v_go(14 + s, far[s], sibling)
-
+            v_copy(6 + 2 * s + part, far[s], sibling, part).wait_recv()
+        v_go(17 + s, far[s], sibling)
+
+    v_go(0, near[0], x_step(1), 0)
+    v_go(3, near[0], x_step(3), 1)
+    v_go(1, near[0], x_step(1), 1)
+    v_go(2, near[0], x_step(3), 0)
+    along_z(0, 0)
+    along_z(0, 1)
+    fetches[3].wait()
+    for r in range(32):
+        pack[pl.ds(r, 8, stride=32), :] = x_ref[:, 128 * r : 128 * r + 128]
     in_start, in_wait, in_sent = exchange(pack, coeffs, 0)
     in_start()
-    for fetch in fetches[1:4]:
-        fetch.wait()
-    fit_potential(v_ref, tabs, planes, own)
-    for column in range(2):
-        v[column, grid] = own[192 * column : 192 * column + 192]
-    for s, step in ((1, 1), (2, 3), (3, 2)):
-        v_go(s - 1, near[0], x_step(step))
-    along_z(0)
+    center = (lower[0] + upper[0]) * 0.5
+    inverse = 1.0 / ((upper[0] - lower[0]) * 0.5)
     for fetch in fetches[4:]:
         fetch.wait()
-    rh, rl = split(rotation_ref[...].T)
-    left[...] = jnp.concatenate([rh, rl, rh, rl], 1)
-    center = (lower[0] + upper[0]) * 0.5
-    inverse = 1.0 / ((upper[0] - lower[0]) * 0.5)
+    from_x(0, 1, 0)
+    v_go(4, near[1], x_step(1), 0)
+    from_x(3, 2, 1)
+    v_go(5, near[2], x_step(3), 1)
+    from_x(1, 1, 1)
+    v_go(14, near[1], sibling)
+    from_x(2, 2, 0)
+    v_go(15, near[2], sibling)
     in_wait()
     c = jnp.concatenate([coeffs[pl.ds(k8, 32, stride=8), :] for k8 in range(8)], 1)
     expand_rows(c, tabs, scratch)
     from_z(0)
-    for s in range(1, 4):
-        from_x(s)
+    from_x(4, 3, 0)
+    from_x(5, 3, 1)
+    v_go(16, near[3], sibling)
     for s in range(1, 4):
         from_z(s)
     cross_planes(core, v, tabs, scratch)
     for s in range(1, 4):
-        v_copy(10 + s, near[s], sibling, None, 1 - core).wait_recv()
+        v_copy(13 + s, near[s], sibling, None, 1 - core).wait_recv()
     for s in range(4):
-        v_copy(14 + s, far[s], sibling, None, 1 - core).wait_recv()
+        v_copy(17 + s, far[s], sibling, None, 1 - core).wait_recv()
     cross_planes(1 - core, v, tabs, scratch)
     shift = kinetic_plane() - center
     first = (shift * c + contract_rows(tabs, scratch)) * inverse
@@ -387,7 +390,7 @@
     out = (2.0 * inverse) * second - c
     for k8 in range(8):
         spread[pl.ds(k8, 32, stride=8), :] = out[:, 128 * k8 : 128 * k8 + 128]
-    out_start, out_wait, out_sent = exchange(spread, landed, SHARDS)
+    out_start, out_wait, out_sent = exchange(spread, landed, 1)
     out_start()
     for copy in sent:
         copy.wait_send()
@@ -396,76 +399,77 @@
     for r in range(32):
         rows = landed[pl.ds(r, 8, stride=32), :]
         x_ref[:, 128 * r : 128 * r + 128] = rows
-        chunk[r] = rows
-
-    def b_copy(d, to, block, slot):
-        return remote(chunk.at[block], blocks.at[slot], b_send.at[d], b_recv.at[d], (to, grid))
-
-    @pl.loop(1, GROUPS)
-    def _(d):
-        to = (band + d) % GROUPS
-        b_copy(d, to, to, band).start()
-
+        chunk[r % 2, r // 2] = rows
     write = pltpu.make_async_copy(x_ref, filtered, local_sem.at[0])
     write.start()
-    blocks[band] = chunk[band]
-
-    @pl.loop(1, GROUPS)
-    def _(d):
-        came = (band + GROUPS - d) % GROUPS
-        b_copy(d, came, came, came).wait_recv()
-
+
+    swap = remote(chunk.at[1 - core], pairs.at[:, core], b_send.at[0], b_recv.at[0], sibling)
+    swap.start()
+    pairs[:, core] = chunk[core]
+    remote(chunk.at[core], pairs.at[:, 1 - core], b_send.at[0], b_recv.at[0], sibling).wait_recv()
+
+    for dz, dy in sorted(
+        ((dz, dy) for dz in range(4) for dy in range(4) if dz + dy),
+        key=lambda d: -2 * min(d[0], 4 - d[0]) - min(d[1], 4 - d[1]),
+    ):
+        to = (z_hi + dz) % 4 * 4 + (y + dy) % 4
+        remote(pairs.at[to], blocks.at[chip], b_send.at[1], b_recv.at[1], (to * 2 + core, grid)).start()
+
+    blocks[chip] = pairs[chip]
+    all_chips = remote(
+        pairs.at[pl.ds(0, CHIPS - 1)], blocks.at[pl.ds(0, CHIPS - 1)], b_send.at[1], b_recv.at[1], sibling
+    )
+    all_chips.wait_recv()
     for s in range(STEPS):
-        gathered[band, pl.ds(8 * s, 8), :] = blocks[owners[s]]
+        gathered[band, pl.ds(8 * s, 8), :] = blocks[owners[s] // 2, owners[s] % 2]
 
     def c_copy(sem, index, to):
         ref = gathered.at[index]
-        return remote(ref, ref, c_send.at[sem], c_recv.at[sem], (to, grid))
-
-    def index_of(dz, dy, other):
-        k = 1 - core if other else core
-        return ((z_hi + 4 - dz) % 4) * 8 + ((y + 4 - dy) % 4) * 2 + k
-
-    away = sibling[0]
-    for dz in range(1, 4):
+        return remote(ref, ref, c_send, c_recv.at[sem], (to, grid))
+
+    def index_of(dz, dy):
+        return ((z_hi + 4 - dz) % 4) * 8 + ((y + 4 - dy) % 4) * 2 + core
+
+    def deliver(index):
+        pltpu.make_async_copy(gathered.at[index], arrived.at[index], local_sem.at[1]).start()
+        remote(gathered.at[index], arrived.at[index], c_send, c_recv.at[0], sibling).start()
+
+    def along_z_hi(dz):
         c_copy(dz, band, ((z_hi + dz) % 4) * 8 + band % 8).start()
-    for dz in range(4):
-        mine = index_of(dz, 0, False)
-        if dz:
-            c_copy(dz, mine, away).wait_recv()
-        for dy in range(1, 4):
+
+    def along_y(dz):
+        mine = index_of(dz, 0)
+        for dy in (1, 3, 2):
             c_copy(4 + 3 * dz + dy - 1, mine, z_hi * 8 + ((y + dy) % 4) * 2 + core).start()
-        c_copy(16 + 4 * dz, mine, away).start()
-    for dz in range(4):
-        for dy in range(1, 4):
-            mine = index_of(dz, dy, False)
-            c_copy(4 + 3 * dz + dy - 1, mine, away).wait_recv()
-            c_copy(16 + 4 * dz + dy, mine, away).start()
-
-    writes = []
-    for dz in range(4):
-        for dy in range(4):
-            c_copy(16 + 4 * dz + dy, index_of(dz, dy, True), away).wait_recv()
-            pair = ((z_hi + 4 - dz) % 4) * 4 + (y + 4 - dy) % 4
-            ah, al = split(jnp.concatenate([gathered[2 * pair], gathered[2 * pair + 1]], 1))
-            at = pl.ds(pl.multiple_of(pair * 256, 256), 256)
-            rotated[:, at] = dot(left[...], jnp.concatenate([ah, ah, al, al], 0))
-            writes.append(pltpu.make_async_copy(rotated.at[:, at], residents.at[:, at], out_sem.at[4 * dz + dy]))
-            writes[-1].start()
-
-    @pl.loop(1, GROUPS)
-    def _(d):
-        to = (band + d) % GROUPS
-        b_copy(d, to, to, band).wait_send()
-
-    @pl.loop(1, 32)
-    def _(d):
-        c_copy(d, band, away).wait_send()
-
+        deliver(mine)
+
+    def from_y(dz):
+        for dy in (1, 3, 2):
+            mine = index_of(dz, dy)
+            c_copy(4 + 3 * dz + dy - 1, mine, sibling[0]).wait_recv()
+            deliver(mine)
+
+    along_z_hi(1)
+    along_z_hi(3)
+    along_y(0)
+    along_z_hi(2)
+    for dz in (1, 3):
+        c_copy(dz, index_of(dz, 0), sibling[0]).wait_recv()
+        along_y(dz)
+    from_y(0)
+    c_copy(2, index_of(2, 0), sibling[0]).wait_recv()
+    along_y(2)
+    for dz in (1, 3, 2):
+        from_y(dz)
+    swap.wait_send()
+    all_chips.wait_send()
     out_sent()
     write.wait()
-    for copy in writes:
-        copy.wait()
+    half = pl.ds(0, CHIPS)
+    pltpu.make_async_copy(gathered.at[half], arrived.at[half], local_sem.at[1]).wait()
+    remote(gathered.at[half], arrived.at[half], c_send, c_recv.at[0], sibling).wait_recv()
+    every = pl.ds(0, GROUPS - 1)
+    remote(gathered.at[every], arrived.at[every], c_send, c_recv.at[0], sibling).wait_send()
 
 
 SMEM = pl.BlockSpec(memory_space=pltpu.SMEM)
@@ -474,14 +478,13 @@
     filter_kernel,
     out_shape=(
         jax.ShapeDtypeStruct((8, 4096), F32),
-        jax.ShapeDtypeStruct((192, 4096), F32),
+        jax.ShapeDtypeStruct((GROUPS, 64, 128), F32),
     ),
-    in_specs=[ANY] * 3 + [SMEM] * 3 + [ANY] * 8,
+    in_specs=[ANY] * 2 + [SMEM] * 3 + [ANY] * 8,
     out_specs=(ANY, ANY),
     scratch_shapes=[
         pltpu.VMEM((8, 4096), F32),
         pltpu.VMEM((12, 9216), F32),
-        pltpu.VMEM((64, 192), F32),
         pltpu.VMEM((64, 128), BF16),
         pltpu.VMEM((128, 512), BF16),
         pltpu.VMEM((192, 256), BF16),
@@ -498,20 +501,18 @@
         pltpu.VMEM((256, 128), F32),
         pltpu.VMEM((256, 128), F32),
         pltpu.VMEM((256, 128), F32),
-        pltpu.VMEM((32, 8, 128), F32),
+        pltpu.VMEM((2, CHIPS, 8, 128), F32),
+        pltpu.VMEM((CHIPS, 2, 8, 128), F32),
         pltpu.VMEM((GROUPS, 64, 128), F32),
-        pltpu.VMEM((GROUPS, 8, 128), F32),
-        pltpu.VMEM((192, 256), BF16),
-        pltpu.VMEM((192, 4096), F32),
-        pltpu.SemaphoreType.DMA((11,)),
-        pltpu.SemaphoreType.DMA((16,)),
-        pltpu.SemaphoreType.DMA((16,)),
-        pltpu.SemaphoreType.DMA((18,)),
-        pltpu.SemaphoreType.DMA((18,)),
-        pltpu.SemaphoreType.DMA((32,)),
-        pltpu.SemaphoreType.DMA((32,)),
-        pltpu.SemaphoreType.DMA((32,)),
-        pltpu.SemaphoreType.DMA((32,)),
+        pltpu.VMEM((CHIPS, 2, 8, 128), F32),
+        pltpu.SemaphoreType.DMA((10,)),
+        pltpu.SemaphoreType.DMA((2,)),
+        pltpu.SemaphoreType.DMA((2,)),
+        pltpu.SemaphoreType.DMA((21,)),
+        pltpu.SemaphoreType.DMA((21,)),
+        pltpu.SemaphoreType.DMA((2,)),
+        pltpu.SemaphoreType.DMA((2,)),
+        pltpu.SemaphoreType.DMA,
         pltpu.SemaphoreType.DMA((16,)),
     ],
     compiler_params=pltpu.CompilerParams(
@@ -521,12 +522,61 @@
 )
 
 
+def rotate_kernel(rotation_hbm, arrived, filtered, filtered_out, residents, rotation, rows, block, rotated, in_sem, out_sem):
+    get_rotation = pltpu.make_async_copy(rotation_hbm, rotation, in_sem.at[0])
+    get_filtered = pltpu.make_async_copy(filtered, block, in_sem.at[1])
+    get_rows = [
+        pltpu.make_async_copy(arrived.at[pl.ds(4 * i, 4)], rows.at[pl.ds(4 * i, 4)], in_sem.at[2 + i])
+        for i in range(8)
+    ]
+    get_rotation.start()
+    for get in get_rows:
+        get.start()
+    get_filtered.start()
+    get_rotation.wait()
+    rh, rl = split(rotation[...].T)
+    left = jnp.concatenate([rh, rl, rh, rl], 1)
+    writes = [pltpu.make_async_copy(block, filtered_out, out_sem.at[8])]
+    for i in range(8):
+        get_rows[i].wait()
+        ah, al = split(jnp.concatenate([rows[4 * i + j] for j in range(4)], 1))
+        at = pl.ds(512 * i, 512)
+        rotated[:, at] = dot(left, jnp.concatenate([ah, ah, al, al], 0))
+        writes.append(pltpu.make_async_copy(rotated.at[:, at], residents.at[:, at], out_sem.at[i]))
+        writes[-1].start()
+        if i == 0:
+            get_filtered.wait()
+            writes[0].start()
+    for write in writes:
+        write.wait()
+
+
+ROTATE = pl.pallas_call(
+    rotate_kernel,
+    out_shape=(
+        jax.ShapeDtypeStruct((8, 4096), F32),
+        jax.ShapeDtypeStruct((192, 4096), F32),
+    ),
+    in_specs=[ANY] * 3,
+    out_specs=(ANY, ANY),
+    scratch_shapes=[
+        pltpu.VMEM((64, 192), F32),
+        pltpu.VMEM((GROUPS, 64, 128), F32),
+        pltpu.VMEM((8, 4096), F32),
+        pltpu.VMEM((192, 4096), F32),
+        pltpu.SemaphoreType.DMA((10,)),
+        pltpu.SemaphoreType.DMA((9,)),
+    ],
+    compiler_params=pltpu.CompilerParams(vmem_limit_bytes=VMEM_LIMIT),
+    name="rotate",
+)
+
+
 def body(block_coeffs, potential, lower_edge, upper_edge, rotation, owners):
     consts = [jnp.asarray(t) for t in tables()]
+    filtered, arrived = FILTER(block_coeffs, potential, lower_edge, upper_edge, owners, *consts)
     coefficients = rotation.transpose(0, 2, 1).reshape(64, 192)
-    return tuple(
-        FILTER(block_coeffs, potential, coefficients, lower_edge, upper_edge, owners, *consts)
-    )
+    return tuple(ROTATE(coefficients, arrived, filtered))
 
 
 def solution(mesh):

time: 64.1 us -> 58.3 us (0.910)
  local copies, waits for them, and re-layouts: 5.42 us -> 0 us
    unnamed x2 -> x0, local copies, waits for them, and re-layouts: 5.42 us -> none
    pallas_call x1 -> x2, Pallas kernels: 56.2 us -> 56.2 us  [the longest x1 52.5 us: body(): FILTER(block_coeffs, potential, lower_edge, upper_edge, owners, *consts)]
where the time goes in v3:
time: 58.3 us; the launch traced here: 58.2 us
  Pallas kernels  56.2 us (96%)
  between operations  1.93 us (3%)
    pallas_call x1, Pallas kernels, body(): FILTER(block_coeffs, potential, lower_edge, upper_edge, owners, *consts)  52.5 us
    pallas_call x1, Pallas kernels, body(): return tuple(ROTATE(coefficients, arrived, filtered))  3.77 us

profile of v3, /device:TPU:1, one launch (start us, length us, event | category | flops | bytes accessed | tf_op | source)
XLA Modules:
  0.0 58.2 jit_solution(5007642568727518005)
XLA Ops:
  1.9 52.5 %filter.1 = (f32[8,4096]{1,0:T(8,128)}, f32[32,64,128]{2,1,0:T(8,128)}) custom-call(f32[8,4096]{1,0:T(8,128)} %x_hbm.1, f32[12,9216]{1,0:T(8,128)} %v_hbm.1, f32[1]{0:T(128)S(6)} %copy.16.lower, f32[1]{0:T(128)S(6)} %copy.17.upper, s32[8]{0:T(128)} %owners.1, bf16[64,128]{1,0:T(8,128)(2,1)} %constant.16.clone.refs_0_, ...), custom_call_target="tpu_custom_call" | custom-call | tf_op jit(solution)/shard_map/filter/pallas_call | solution.py:577
  54.4 3.8 %rotate.1 = (f32[8,4096]{1,0:T(8,128)}, f32[192,4096]{1,0:T(8,128)}) custom-call(f32[64,192]{1,0:T(8,128)} %bitcast.3, f32[32,64,128]{2,1,0:T(8,128)} %get-tuple-element.4.arrived, f32[8,4096]{1,0:T(8,128)} %get-tuple-element.5.filtered), custom_call_target="tpu_custom_call" | custom-call | tf_op jit(solution)/shard_map/rotate/pallas_call | solution.py:579

commit v4 on v3

--- a/solution.py
+++ b/solution.py
@@ -138,14 +138,12 @@
     lane = lax.broadcasted_iota(jnp.int32, (32, 128), 1)
     low = lane < 64
     blank = jnp.zeros((4, 384), F32)
-    for i in range(4):
-        blocks = []
-        for c in range(6 * i, 6 * i + 6):
-            blocks += [v_ref[:, 384 * c : 384 * c + 384], blank]
-        rows = jnp.concatenate(blocks, 0)
-        fit = twofold(rows, z_fit, 256)
-        for tile in range(2):
-            planes[tile, pl.ds(96 * i, 96), :] = fit[:, 128 * tile : 128 * tile + 128]
+    blocks = []
+    for c in range(24):
+        blocks += [v_ref[:, 384 * c : 384 * c + 384], blank]
+    fit = twofold(jnp.concatenate(blocks, 0), z_fit, 256)
+    for tile in range(2):
+        planes[tile] = fit[:, 128 * tile : 128 * tile + 128]
     columns = []
     for n in range(0, 12, 2):
         parts = []
@@ -234,13 +232,13 @@
 ]
 
 
-def filter_kernel(x_hbm, v_hbm, lower, upper, owners, *refs):
+def filter_kernel(x_hbm, v_hbm, rotation_hbm, lower, upper, owners, *refs):
     tables_hbm = refs[:8]
-    filtered, arrived = refs[8:10]
+    filtered, residents = refs[8:10]
     x_ref, v_ref = refs[10:12]
     tabs = refs[12:20]
     scratch = refs[20:24]
-    (v, planes, own, pack, coeffs, spread, landed, chunk, pairs, gathered, blocks, local_sem,
+    (v, planes, own, pack, coeffs, spread, landed, pairs, mate, gathered, blocks, rotation_ref, left, rotated, local_sem,
      a_send, a_recv, v_send, v_recv, b_send, b_recv, c_send, c_recv) = refs[24:]
     band = lax.axis_index("band")
     grid = lax.axis_index("grid")
@@ -248,9 +246,9 @@
     z_lo, x = grid // 4, grid % 4
     sibling = (z_hi * 8 + y * 2 + 1 - core, grid)
 
-    def z_step(step):
+    def z_step(step, other=0):
         z = (z_hi * 2 + z_lo + step) % 8
-        return ((z // 2) * 8 + band % 8, (1 - z_lo) * 4 + x)
+        return ((z // 2) * 8 + y * 2 + (core + other) % 2, (1 - z_lo) * 4 + x)
 
     def x_step(step):
         return (band, z_lo * 4 + (x + step) % 4)
@@ -263,8 +261,8 @@
             src_ref=src, dst_ref=dst, send_sem=send, recv_sem=recv, device_id=to, device_id_type=MESH
         )
 
-    sources = (v_hbm, tables_hbm[6], tables_hbm[7], x_hbm) + tuple(tables_hbm[:6])
-    targets = (v_ref, tabs[6], tabs[7], x_ref) + tuple(tabs[:6])
+    sources = (v_hbm, tables_hbm[6], tables_hbm[7], x_hbm, rotation_hbm) + tuple(tables_hbm[:6])
+    targets = (v_ref, tabs[6], tabs[7], x_ref, rotation_ref) + tuple(tabs[:6])
     fetches = [
         pltpu.make_async_copy(src, dst, local_sem.at[i])
         for i, (src, dst) in enumerate(zip(sources, targets))
@@ -280,41 +278,35 @@
     @pl.loop(1, SHARDS)
     def _(d):
         greet((band, (grid + d) % SHARDS))
+        greet((sibling[0], (grid + d) % SHARDS))
 
     @pl.loop(1, CHIPS)
     def _(d):
         greet((((chip + d) % CHIPS) * 2 + core, grid))
 
     greet(sibling)
-    greet(z_step(1))
-    greet(z_step(7))
+    for other in range(2):
+        greet(z_step(1, other))
+        greet(z_step(7, other))
 
     for fetch in fetches[:3]:
         fetch.wait()
     fit_potential(v_ref, tabs, planes, own)
     for column in range(2):
         v[column, grid] = own[192 * column : 192 * column + 192]
-    pl.semaphore_wait(barrier, SHARDS - 1 + CHIPS - 1 + 3)
-
-    def exchange(src, dst, sem):
-        def copy(to, block, slot, rows=32):
-            return remote(
-                src.at[pl.ds(pl.multiple_of(block * 32, 32), rows), :],
-                dst.at[pl.ds(pl.multiple_of(slot * 32, 32), rows), :],
-                a_send.at[sem], a_recv.at[sem], (band, to),
-            )
-
-        def start():
-            for dz, dx in ((1, 2), (1, 1), (1, 3), (0, 2), (1, 0), (0, 1), (0, 3)):
-                to = (z_lo + dz) % 2 * 4 + (x + dx) % 4
-                copy(to, to, grid).start()
-            own = pl.ds(pl.multiple_of(grid * 32, 32), 32)
-            dst[own, :] = src[own, :]
-
-        def all_of_them():
-            return copy((grid + 1) % SHARDS, 0, 0, 32 * (SHARDS - 1))
-
-        return start, all_of_them().wait_recv, all_of_them().wait_send
+    pl.semaphore_wait(barrier, 2 * (SHARDS - 1) + CHIPS - 1 + 5)
+
+    def rows_of(ref, block, size):
+        return ref.at[pl.ds(pl.multiple_of(block * size, size), size), :]
+
+    def bring(to, block, slot):
+        return remote(
+            rows_of(pack, block, 32), rows_of(coeffs, slot, 32), a_send.at[0], a_recv.at[0], (band, to)
+        )
+
+    def all_rows(ref, sem):
+        count = pl.ds(0, 224 if sem == 0 else 240)
+        return remote(ref.at[count, :], ref.at[count, :], a_send.at[sem], a_recv.at[sem], sibling)
 
     near = [z_lo * 4 + (x + s) % 4 for s in (0, 3, 1, 2)]
     far = [(1 - z_lo) * 4 + (x + s) % 4 for s in (0, 3, 1, 2)]
@@ -337,6 +329,11 @@
     def from_x(sem, s, part):
         v_copy(sem, near[s], sibling, part).wait_recv()
         along_z(s, part)
+
+    def last_along_z(part):
+        v_copy(4 + part, near[3], sibling, part).wait_recv()
+        along_z(3, part)
+        v_go(20 + part, near[3], z_step(7 if part else 1, 1), part)
 
     def from_z(s):
         for part in range(2):
@@ -352,34 +349,42 @@
     fetches[3].wait()
     for r in range(32):
         pack[pl.ds(r, 8, stride=32), :] = x_ref[:, 128 * r : 128 * r + 128]
-    in_start, in_wait, in_sent = exchange(pack, coeffs, 0)
-    in_start()
     center = (lower[0] + upper[0]) * 0.5
     inverse = 1.0 / ((upper[0] - lower[0]) * 0.5)
     for fetch in fetches[4:]:
         fetch.wait()
+    rh, rl = split(rotation_ref[...].T)
+    left[...] = jnp.concatenate([rh, rl, rh, rl], 1)
     from_x(0, 1, 0)
     v_go(4, near[1], x_step(1), 0)
     from_x(3, 2, 1)
     v_go(5, near[2], x_step(3), 1)
+    for d in range(1, SHARDS):
+        to = (grid + d) % SHARDS
+        bring(to, to, grid).start()
+    rows_of(coeffs, grid, 32)[...] = rows_of(pack, grid, 32)[...]
     from_x(1, 1, 1)
     v_go(14, near[1], sibling)
     from_x(2, 2, 0)
     v_go(15, near[2], sibling)
-    in_wait()
+    from_z(0)
+    last_along_z(0)
+    last_along_z(1)
+    v_go(16, near[3], sibling)
+    from_z(1)
+    from_z(2)
+    all_rows(coeffs, 0).wait_recv()
     c = jnp.concatenate([coeffs[pl.ds(k8, 32, stride=8), :] for k8 in range(8)], 1)
     expand_rows(c, tabs, scratch)
-    from_z(0)
-    from_x(4, 3, 0)
-    from_x(5, 3, 1)
-    v_go(16, near[3], sibling)
-    for s in range(1, 4):
-        from_z(s)
+    for part in range(2):
+        v_copy(12 + part, far[3], sibling, part).wait_recv()
     cross_planes(core, v, tabs, scratch)
     for s in range(1, 4):
         v_copy(13 + s, near[s], sibling, None, 1 - core).wait_recv()
-    for s in range(4):
+    for s in range(3):
         v_copy(17 + s, far[s], sibling, None, 1 - core).wait_recv()
+    for part in range(2):
+        v_copy(20 + part, far[3], sibling, part, 1 - core).wait_recv()
     cross_planes(1 - core, v, tabs, scratch)
     shift = kinetic_plane() - center
     first = (shift * c + contract_rows(tabs, scratch)) * inverse
@@ -388,25 +393,30 @@
     cross_planes(1, v, tabs, scratch)
     second = shift * first + contract_rows(tabs, scratch)
     out = (2.0 * inverse) * second - c
+    all_rows(coeffs, 0).wait_send()
     for k8 in range(8):
-        spread[pl.ds(k8, 32, stride=8), :] = out[:, 128 * k8 : 128 * k8 + 128]
-    out_start, out_wait, out_sent = exchange(spread, landed, 1)
-    out_start()
+        pack[pl.ds(k8, 32, stride=8), :] = out[:, 128 * k8 : 128 * k8 + 128]
+    for k in range(2):
+        spread[pl.ds(128 * k, 128), :] = pack[pl.ds(k, 128, stride=2), :]
+
+    def bring_back(to, other):
+        k = 1 - core if other else core
+        return remote(
+            rows_of(spread, k * 8 + to, 16), rows_of(landed, core * 8 + grid, 16),
+            a_send.at[1], a_recv.at[1], (chip * 2 + k, to),
+        )
+
+    for d in range(1, SHARDS):
+        for other in range(2):
+            bring_back((grid + d) % SHARDS, other).start()
+    bring_back(grid, 1).start()
+    rows_of(landed, core * 8 + grid, 16)[...] = rows_of(spread, core * 8 + grid, 16)[...]
     for copy in sent:
         copy.wait_send()
-    in_sent()
-    out_wait()
-    for r in range(32):
-        rows = landed[pl.ds(r, 8, stride=32), :]
-        x_ref[:, 128 * r : 128 * r + 128] = rows
-        chunk[r % 2, r // 2] = rows
-    write = pltpu.make_async_copy(x_ref, filtered, local_sem.at[0])
-    write.start()
-
-    swap = remote(chunk.at[1 - core], pairs.at[:, core], b_send.at[0], b_recv.at[0], sibling)
-    swap.start()
-    pairs[:, core] = chunk[core]
-    remote(chunk.at[core], pairs.at[:, 1 - core], b_send.at[0], b_recv.at[0], sibling).wait_recv()
+    all_rows(landed, 1).wait_recv()
+    for k in range(2):
+        for i in range(CHIPS):
+            pairs[i, k] = landed[pl.ds(128 * k + i, 8, stride=16), :]
 
     for dz, dy in sorted(
         ((dz, dy) for dz in range(4) for dy in range(4) if dz + dy),
@@ -416,6 +426,8 @@
         remote(pairs.at[to], blocks.at[chip], b_send.at[1], b_recv.at[1], (to * 2 + core, grid)).start()
 
     blocks[chip] = pairs[chip]
+    swap = remote(pairs.at[:, 1 - core], mate, b_send.at[0], b_recv.at[0], sibling)
+    swap.start()
     all_chips = remote(
         pairs.at[pl.ds(0, CHIPS - 1)], blocks.at[pl.ds(0, CHIPS - 1)], b_send.at[1], b_recv.at[1], sibling
     )
@@ -430,9 +442,8 @@
     def index_of(dz, dy):
         return ((z_hi + 4 - dz) % 4) * 8 + ((y + 4 - dy) % 4) * 2 + core
 
-    def deliver(index):
-        pltpu.make_async_copy(gathered.at[index], arrived.at[index], local_sem.at[1]).start()
-        remote(gathered.at[index], arrived.at[index], c_send, c_recv.at[0], sibling).start()
+    def deliver(dz, dy):
+        c_copy(16 + 4 * dz + dy, index_of(dz, dy), sibling[0]).start()
 
     def along_z_hi(dz):
         c_copy(dz, band, ((z_hi + dz) % 4) * 8 + band % 8).start()
@@ -441,13 +452,22 @@
         mine = index_of(dz, 0)
         for dy in (1, 3, 2):
             c_copy(4 + 3 * dz + dy - 1, mine, z_hi * 8 + ((y + dy) % 4) * 2 + core).start()
-        deliver(mine)
+        deliver(dz, 0)
 
     def from_y(dz):
         for dy in (1, 3, 2):
-            mine = index_of(dz, dy)
-            c_copy(4 + 3 * dz + dy - 1, mine, sibling[0]).wait_recv()
-            deliver(mine)
+            c_copy(4 + 3 * dz + dy - 1, index_of(dz, dy), sibling[0]).wait_recv()
+            deliver(dz, dy)
+
+    def rotate(dz):
+        for dy in range(4):
+            twin = index_of(dz, dy) + 1 - 2 * core
+            c_copy(16 + 4 * dz + dy, twin, sibling[0]).wait_recv()
+        level = (z_hi + 4 - dz) % 4
+        ah, al = split(jnp.concatenate([gathered[level * 8 + i] for i in range(8)], 1))
+        at = pl.ds(pl.multiple_of(level * 1024, 1024), 1024)
+        rotated[:, at] = dot(left[...], jnp.concatenate([ah, ah, al, al], 0))
+        return pltpu.make_async_copy(rotated.at[:, at], residents.at[:, at], local_sem.at[1 + dz])
 
     along_z_hi(1)
     along_z_hi(3)
@@ -456,20 +476,35 @@
     for dz in (1, 3):
         c_copy(dz, index_of(dz, 0), sibling[0]).wait_recv()
         along_y(dz)
+    swap.wait_recv()
+    for i in range(CHIPS):
+        x_ref[:, pl.ds(pl.multiple_of(256 * i + 128 * core, 128), 128)] = pairs[i, core]
+        x_ref[:, pl.ds(pl.multiple_of(256 * i + 128 - 128 * core, 128), 128)] = mate[i]
+    write = pltpu.make_async_copy(x_ref, filtered, local_sem.at[0])
+    write.start()
     from_y(0)
     c_copy(2, index_of(2, 0), sibling[0]).wait_recv()
     along_y(2)
-    for dz in (1, 3, 2):
-        from_y(dz)
+    writes = [write]
+
+    def finish(dz):
+        writes.append(rotate(dz))
+        writes[-1].start()
+
+    finish(0)
+    from_y(1)
+    from_y(3)
+    finish(1)
+    from_y(2)
+    finish(3)
+    finish(2)
+    all_chips.wait_send()
+    all_rows(landed, 1).wait_send()
     swap.wait_send()
-    all_chips.wait_send()
-    out_sent()
-    write.wait()
-    half = pl.ds(0, CHIPS)
-    pltpu.make_async_copy(gathered.at[half], arrived.at[half], local_sem.at[1]).wait()
-    remote(gathered.at[half], arrived.at[half], c_send, c_recv.at[0], sibling).wait_recv()
     every = pl.ds(0, GROUPS - 1)
-    remote(gathered.at[every], arrived.at[every], c_send, c_recv.at[0], sibling).wait_send()
+    remote(gathered.at[every], gathered.at[every], c_send, c_recv.at[0], sibling).wait_send()
+    for copy in writes:
+        copy.wait()
 
 
 SMEM = pl.BlockSpec(memory_space=pltpu.SMEM)
@@ -478,9 +513,9 @@
     filter_kernel,
     out_shape=(
         jax.ShapeDtypeStruct((8, 4096), F32),
-        jax.ShapeDtypeStruct((GROUPS, 64, 128), F32),
+        jax.ShapeDtypeStruct((192, 4096), F32),
     ),
-    in_specs=[ANY] * 2 + [SMEM] * 3 + [ANY] * 8,
+    in_specs=[ANY] * 3 + [SMEM] * 3 + [ANY] * 8,
     out_specs=(ANY, ANY),
     scratch_shapes=[
         pltpu.VMEM((8, 4096), F32),
@@ -501,19 +536,22 @@
         pltpu.VMEM((256, 128), F32),
         pltpu.VMEM((256, 128), F32),
         pltpu.VMEM((256, 128), F32),
-        pltpu.VMEM((2, CHIPS, 8, 128), F32),
         pltpu.VMEM((CHIPS, 2, 8, 128), F32),
+        pltpu.VMEM((CHIPS, 8, 128), F32),
         pltpu.VMEM((GROUPS, 64, 128), F32),
         pltpu.VMEM((CHIPS, 2, 8, 128), F32),
-        pltpu.SemaphoreType.DMA((10,)),
+        pltpu.VMEM((64, 192), F32),
+        pltpu.VMEM((192, 256), BF16),
+        pltpu.VMEM((192, 4096), F32),
+        pltpu.SemaphoreType.DMA((11,)),
         pltpu.SemaphoreType.DMA((2,)),
         pltpu.SemaphoreType.DMA((2,)),
-        pltpu.SemaphoreType.DMA((21,)),
-        pltpu.SemaphoreType.DMA((21,)),
+        pltpu.SemaphoreType.DMA((22,)),
+        pltpu.SemaphoreType.DMA((22,)),
         pltpu.SemaphoreType.DMA((2,)),
         pltpu.SemaphoreType.DMA((2,)),
         pltpu.SemaphoreType.DMA,
-        pltpu.SemaphoreType.DMA((16,)),
+        pltpu.SemaphoreType.DMA((32,)),
     ],
     compiler_params=pltpu.CompilerParams(
         collective_id=0, has_side_effects=True, vmem_limit_bytes=VMEM_LIMIT
@@ -522,61 +560,47 @@
 )
 
 
-def rotate_kernel(rotation_hbm, arrived, filtered, filtered_out, residents, rotation, rows, block, rotated, in_sem, out_sem):
-    get_rotation = pltpu.make_async_copy(rotation_hbm, rotation, in_sem.at[0])
-    get_filtered = pltpu.make_async_copy(filtered, block, in_sem.at[1])
-    get_rows = [
-        pltpu.make_async_copy(arrived.at[pl.ds(4 * i, 4)], rows.at[pl.ds(4 * i, 4)], in_sem.at[2 + i])
-        for i in range(8)
-    ]
-    get_rotation.start()
-    for get in get_rows:
-        get.start()
-    get_filtered.start()
-    get_rotation.wait()
-    rh, rl = split(rotation[...].T)
-    left = jnp.concatenate([rh, rl, rh, rl], 1)
-    writes = [pltpu.make_async_copy(block, filtered_out, out_sem.at[8])]
+def write_kernel(filtered, residents, filtered_out, residents_out, block, rows, in_sem, out_sem):
+    parts = [(filtered, block, filtered_out)]
     for i in range(8):
-        get_rows[i].wait()
-        ah, al = split(jnp.concatenate([rows[4 * i + j] for j in range(4)], 1))
-        at = pl.ds(512 * i, 512)
-        rotated[:, at] = dot(left, jnp.concatenate([ah, ah, al, al], 0))
-        writes.append(pltpu.make_async_copy(rotated.at[:, at], residents.at[:, at], out_sem.at[i]))
-        writes[-1].start()
-        if i == 0:
-            get_filtered.wait()
-            writes[0].start()
+        at = pl.ds(24 * i, 24)
+        parts.append((residents.at[at, :], rows.at[at, :], residents_out.at[at, :]))
+    reads = [pltpu.make_async_copy(a, b, in_sem.at[i]) for i, (a, b, _) in enumerate(parts)]
+    writes = [pltpu.make_async_copy(b, c, out_sem.at[i]) for i, (_, b, c) in enumerate(parts)]
+    for read in reads:
+        read.start()
+    for read, write in zip(reads, writes):
+        read.wait()
+        write.start()
     for write in writes:
         write.wait()
 
 
-ROTATE = pl.pallas_call(
-    rotate_kernel,
+WRITE = pl.pallas_call(
+    write_kernel,
     out_shape=(
         jax.ShapeDtypeStruct((8, 4096), F32),
         jax.ShapeDtypeStruct((192, 4096), F32),
     ),
-    in_specs=[ANY] * 3,
+    in_specs=[ANY] * 2,
     out_specs=(ANY, ANY),
     scratch_shapes=[
-        pltpu.VMEM((64, 192), F32),
-        pltpu.VMEM((GROUPS, 64, 128), F32),
         pltpu.VMEM((8, 4096), F32),
         pltpu.VMEM((192, 4096), F32),
-        pltpu.SemaphoreType.DMA((10,)),
+        pltpu.SemaphoreType.DMA((9,)),
         pltpu.SemaphoreType.DMA((9,)),
     ],
     compiler_params=pltpu.CompilerParams(vmem_limit_bytes=VMEM_LIMIT),
-    name="rotate",
+    name="write",
 )
 
 
 def body(block_coeffs, potential, lower_edge, upper_edge, rotation, owners):
     consts = [jnp.asarray(t) for t in tables()]
-    filtered, arrived = FILTER(block_coeffs, potential, lower_edge, upper_edge, owners, *consts)
     coefficients = rotation.transpose(0, 2, 1).reshape(64, 192)
-    return tuple(ROTATE(coefficients, arrived, filtered))
+    return tuple(
+        WRITE(*FILTER(block_coeffs, potential, coefficients, lower_edge, upper_edge, owners, *consts))
+    )
 
 
 def solution(mesh):

time: 58.3 us -> 55.6 us (0.954)
  Pallas kernels: 56.2 us -> 53.5 us
    pallas_call x2, Pallas kernels: 56.2 us -> 53.5 us  [the longest x1 50.6 us: body(): FILTER(block_coeffs, potential, coefficients, lower_edge, upper_edge, own...]
where the time goes in v4:
time: 55.6 us; the launch traced here: 55.4 us
  Pallas kernels  53.5 us (96%)
  between operations  1.93 us (3%)
    pallas_call x1, Pallas kernels, body(): FILTER(block_coeffs, potential, coefficients, lower_edge, upper_edge, own...  50.6 us
    pallas_call x1, Pallas kernels, body(): WRITE(*FILTER(block_coeffs, potential, coefficients, lower_edge, upper_ed...  2.88 us

profile of v4, /device:TPU:1, one launch (start us, length us, event | category | flops | bytes accessed | tf_op | source)
XLA Modules:
  0.0 55.4 jit_solution(16128460768953698706)
XLA Ops:
  1.9 50.6 %filter.1 = (f32[8,4096]{1,0:T(8,128)}, f32[192,4096]{1,0:T(8,128)}) custom-call(f32[8,4096]{1,0:T(8,128)} %x_hbm.1, f32[12,9216]{1,0:T(8,128)} %v_hbm.1, f32[64,192]{1,0:T(8,128)} %bitcast.3, f32[1]{0:T(128)S(6)} %copy.16.lower, f32[1]{0:T(128)S(6)} %copy.17.upper, s32[8]{0:T(128)} %owners.1, bf16[64,128]{1,0:T(8,128)(2,1)} %constant.16.clone.refs_0_, ...), custom_call_target="tpu_custom_call" | custom-call | tf_op jit(solution)/shard_map/filter/pallas_call | solution.py:602
  52.6 2.9 %write.1 = (f32[8,4096]{1,0:T(8,128)}, f32[192,4096]{1,0:T(8,128)}) custom-call(f32[8,4096]{1,0:T(8,128)} %get-tuple-element.4.filtered, f32[192,4096]{1,0:T(8,128)} %get-tuple-element.5.residents), custom_call_target="tpu_custom_call" | custom-call | tf_op jit(solution)/shard_map/write/pallas_call | solution.py:602

commit v5 on v4

--- a/solution.py
+++ b/solution.py
@@ -17,6 +17,7 @@
 GROUPS = 32
 CHIPS = 16
 STEPS = 8
+CORNERS = (2,)
 edge_energy = 1.3
 
 F32 = jnp.float32
@@ -238,8 +239,8 @@
     x_ref, v_ref = refs[10:12]
     tabs = refs[12:20]
     scratch = refs[20:24]
-    (v, planes, own, pack, coeffs, spread, landed, pairs, mate, gathered, blocks, rotation_ref, left, rotated, local_sem,
-     a_send, a_recv, v_send, v_recv, b_send, b_recv, c_send, c_recv) = refs[24:]
+    (v, planes, own, pack, coeffs, spread, landed, pairs, mate, gathered, blocks, relay, rotation_ref, left, rotated, local_sem,
+     a_send, a_recv, v_send, v_recv, b_send, b_recv, c_send, c_recv, news) = refs[24:]
     band = lax.axis_index("band")
     grid = lax.axis_index("grid")
     z_hi, y, core, chip = band // 8, (band // 2) % 4, band % 2, band // 2
@@ -271,30 +272,25 @@
         fetch.start()
 
     barrier = pltpu.get_barrier_semaphore()
-
-    def greet(to):
+    neighbours = [z_step(step, other) for step in (1, 7) for other in range(2)]
+    neighbours += [x_step(1), x_step(3), y_step(1), y_step(3), sibling]
+    for to in neighbours:
         pl.semaphore_signal(barrier, inc=1, device_id=to, device_id_type=MESH)
 
-    @pl.loop(1, SHARDS)
-    def _(d):
-        greet((band, (grid + d) % SHARDS))
-        greet((sibling[0], (grid + d) % SHARDS))
-
-    @pl.loop(1, CHIPS)
-    def _(d):
-        greet((((chip + d) % CHIPS) * 2 + core, grid))
-
-    greet(sibling)
-    for other in range(2):
-        greet(z_step(1, other))
-        greet(z_step(7, other))
+    def tell(turn):
+        for to in (y_step(1), y_step(3)) if turn == 0 else (z_step(1), z_step(7)):
+            pl.semaphore_signal(news.at[turn], inc=1, device_id=to, device_id_type=MESH)
+
+    def hear(turn):
+        pl.semaphore_wait(news.at[turn], 2)
 
     for fetch in fetches[:3]:
         fetch.wait()
     fit_potential(v_ref, tabs, planes, own)
     for column in range(2):
         v[column, grid] = own[192 * column : 192 * column + 192]
-    pl.semaphore_wait(barrier, 2 * (SHARDS - 1) + CHIPS - 1 + 5)
+    pl.semaphore_wait(barrier, len(neighbours))
+    tell(0)
 
     def rows_of(ref, block, size):
         return ref.at[pl.ds(pl.multiple_of(block * size, size), size), :]
@@ -349,6 +345,11 @@
     fetches[3].wait()
     for r in range(32):
         pack[pl.ds(r, 8, stride=32), :] = x_ref[:, 128 * r : 128 * r + 128]
+    partner = (1 - z_lo) * 4 + x
+    by_z = remote(
+        rows_of(pack, (1 - z_lo) * 4 + (x + 2) % 4, 32), relay, a_send.at[2], a_recv.at[2], (band, partner)
+    )
+    by_z.start()
     center = (lower[0] + upper[0]) * 0.5
     inverse = 1.0 / ((upper[0] - lower[0]) * 0.5)
     for fetch in fetches[4:]:
@@ -359,18 +360,26 @@
     v_go(4, near[1], x_step(1), 0)
     from_x(3, 2, 1)
     v_go(5, near[2], x_step(3), 1)
-    for d in range(1, SHARDS):
-        to = (grid + d) % SHARDS
+    hear(0)
+    tell(1)
+    for dz, dx in ((0, 2), (1, 1), (1, 3), (1, 0), (0, 1), (0, 3)):
+        to = (z_lo + dz) % 2 * 4 + (x + dx) % 4
         bring(to, to, grid).start()
     rows_of(coeffs, grid, 32)[...] = rows_of(pack, grid, 32)[...]
+    by_z.wait_recv()
+    remote(
+        relay, rows_of(coeffs, partner, 32), a_send.at[0], a_recv.at[0], (band, z_lo * 4 + (x + 2) % 4)
+    ).start()
     from_x(1, 1, 1)
     v_go(14, near[1], sibling)
     from_x(2, 2, 0)
     v_go(15, near[2], sibling)
     from_z(0)
+    hear(1)
     last_along_z(0)
     last_along_z(1)
     v_go(16, near[3], sibling)
+    tell(2)
     from_z(1)
     from_z(2)
     all_rows(coeffs, 0).wait_recv()
@@ -378,6 +387,8 @@
     expand_rows(c, tabs, scratch)
     for part in range(2):
         v_copy(12 + part, far[3], sibling, part).wait_recv()
+    hear(2)
+    tell(3)
     cross_planes(core, v, tabs, scratch)
     for s in range(1, 4):
         v_copy(13 + s, near[s], sibling, None, 1 - core).wait_recv()
@@ -388,12 +399,15 @@
     cross_planes(1 - core, v, tabs, scratch)
     shift = kinetic_plane() - center
     first = (shift * c + contract_rows(tabs, scratch)) * inverse
+    hear(3)
+    tell(4)
     expand_rows(first, tabs, scratch)
     cross_planes(0, v, tabs, scratch)
     cross_planes(1, v, tabs, scratch)
     second = shift * first + contract_rows(tabs, scratch)
     out = (2.0 * inverse) * second - c
     all_rows(coeffs, 0).wait_send()
+    by_z.wait_send()
     for k8 in range(8):
         pack[pl.ds(k8, 32, stride=8), :] = out[:, 128 * k8 : 128 * k8 + 128]
     for k in range(2):
@@ -418,6 +432,8 @@
         for i in range(CHIPS):
             pairs[i, k] = landed[pl.ds(128 * k + i, 8, stride=16), :]
 
+    hear(4)
+
     for dz, dy in sorted(
         ((dz, dy) for dz in range(4) for dy in range(4) if dz + dy),
         key=lambda d: -2 * min(d[0], 4 - d[0]) - min(d[1], 4 - d[1]),
@@ -450,13 +466,18 @@
 
     def along_y(dz):
         mine = index_of(dz, 0)
-        for dy in (1, 3, 2):
+        for dy in (1, 3) if dz in CORNERS else (2, 1, 3):
             c_copy(4 + 3 * dz + dy - 1, mine, z_hi * 8 + ((y + dy) % 4) * 2 + core).start()
         deliver(dz, 0)
 
     def from_y(dz):
         for dy in (1, 3, 2):
             c_copy(4 + 3 * dz + dy - 1, index_of(dz, dy), sibling[0]).wait_recv()
+            if dz == 0 and dy == 2:
+                for corner in CORNERS:
+                    c_copy(
+                        4 + 3 * corner + 1, index_of(0, 2), ((z_hi + corner) % 4) * 8 + band % 8
+                    ).start()
             deliver(dz, dy)
 
     def rotate(dz):
@@ -464,10 +485,20 @@
             twin = index_of(dz, dy) + 1 - 2 * core
             c_copy(16 + 4 * dz + dy, twin, sibling[0]).wait_recv()
         level = (z_hi + 4 - dz) % 4
-        ah, al = split(jnp.concatenate([gathered[level * 8 + i] for i in range(8)], 1))
-        at = pl.ds(pl.multiple_of(level * 1024, 1024), 1024)
+        return columns_of(level * 8, 8, 1 + dz)
+
+    def rotate_pair(dz, dy):
+        twin = index_of(dz, dy) + 1 - 2 * core
+        c_copy(16 + 4 * dz + dy, twin, sibling[0]).wait_recv()
+        return columns_of(twin // 2 * 2, 2, 3 if dy == 0 else 4 + dy)
+
+    def columns_of(first, count, sem):
+        ah, al = split(jnp.concatenate([gathered[first + i] for i in range(count)], 1))
+        at = pl.ds(pl.multiple_of(first * 128, 256), 128 * count)
         rotated[:, at] = dot(left[...], jnp.concatenate([ah, ah, al, al], 0))
-        return pltpu.make_async_copy(rotated.at[:, at], residents.at[:, at], local_sem.at[1 + dz])
+        write = pltpu.make_async_copy(rotated.at[:, at], residents.at[:, at], local_sem.at[sem])
+        write.start()
+        writes.append(write)
 
     along_z_hi(1)
     along_z_hi(3)
@@ -486,18 +517,14 @@
     c_copy(2, index_of(2, 0), sibling[0]).wait_recv()
     along_y(2)
     writes = [write]
-
-    def finish(dz):
-        writes.append(rotate(dz))
-        writes[-1].start()
-
-    finish(0)
+    rotate(0)
     from_y(1)
     from_y(3)
-    finish(1)
+    rotate(1)
     from_y(2)
-    finish(3)
-    finish(2)
+    rotate(3)
+    for dy in (0, 1, 3, 2):
+        rotate_pair(2, dy)
     all_chips.wait_send()
     all_rows(landed, 1).wait_send()
     swap.wait_send()
@@ -540,18 +567,20 @@
         pltpu.VMEM((CHIPS, 8, 128), F32),
         pltpu.VMEM((GROUPS, 64, 128), F32),
         pltpu.VMEM((CHIPS, 2, 8, 128), F32),
+        pltpu.VMEM((32, 128), F32),
         pltpu.VMEM((64, 192), F32),
         pltpu.VMEM((192, 256), BF16),
         pltpu.VMEM((192, 4096), F32),
         pltpu.SemaphoreType.DMA((11,)),
-        pltpu.SemaphoreType.DMA((2,)),
-        pltpu.SemaphoreType.DMA((2,)),
+        pltpu.SemaphoreType.DMA((3,)),
+        pltpu.SemaphoreType.DMA((3,)),
         pltpu.SemaphoreType.DMA((22,)),
         pltpu.SemaphoreType.DMA((22,)),
         pltpu.SemaphoreType.DMA((2,)),
         pltpu.SemaphoreType.DMA((2,)),
         pltpu.SemaphoreType.DMA,
         pltpu.SemaphoreType.DMA((32,)),
+        pltpu.SemaphoreType.REGULAR((5,)),
     ],
     compiler_params=pltpu.CompilerParams(
         collective_id=0, has_side_effects=True, vmem_limit_bytes=VMEM_LIMIT

time: 55.6 us -> 54.2 us (0.975)
  Pallas kernels: 53.5 us -> 52.1 us
    pallas_call x1, Pallas kernels: 50.6 us -> 49.2 us  [body(): FILTER(block_coeffs, potential, coefficients, lower_edge, upper_edge, own...]
where the time goes in v5:
time: 54.2 us; the launch traced here: 54.1 us
  Pallas kernels  52.1 us (96%)
  between operations  1.93 us (4%)
    pallas_call x1, Pallas kernels, body(): FILTER(block_coeffs, potential, coefficients, lower_edge, upper_edge, own...  49.2 us
    pallas_call x1, Pallas kernels, body(): WRITE(*FILTER(block_coeffs, potential, coefficients, lower_edge, upper_ed...  2.88 us

profile of v5, /device:TPU:1, one launch (start us, length us, event | category | flops | bytes accessed | tf_op | source)
XLA Modules:
  0.0 54.1 jit_solution(9887263774340448826)
XLA Ops:
  1.9 49.2 %filter.1 = (f32[8,4096]{1,0:T(8,128)}, f32[192,4096]{1,0:T(8,128)}) custom-call(f32[8,4096]{1,0:T(8,128)} %x_hbm.1, f32[12,9216]{1,0:T(8,128)} %v_hbm.1, f32[64,192]{1,0:T(8,128)} %bitcast.3, f32[1]{0:T(128)S(6)} %copy.16.lower, f32[1]{0:T(128)S(6)} %copy.17.upper, s32[8]{0:T(128)} %owners.1, bf16[64,128]{1,0:T(8,128)(2,1)} %constant.16.clone.refs_0_, ...), custom_call_target="tpu_custom_call" | custom-call | tf_op jit(solution)/shard_map/filter/pallas_call | solution.py:631
  51.2 2.9 %write.1 = (f32[8,4096]{1,0:T(8,128)}, f32[192,4096]{1,0:T(8,128)}) custom-call(f32[8,4096]{1,0:T(8,128)} %get-tuple-element.4.filtered, f32[192,4096]{1,0:T(8,128)} %get-tuple-element.5.residents), custom_call_target="tpu_custom_call" | custom-call | tf_op jit(solution)/shard_map/write/pallas_call | solution.py:631

commit v6 on v5

--- a/solution.py
+++ b/solution.py
@@ -61,6 +61,11 @@
     return table / NS
 
 
+def block_tiles(hi, lo):
+    blank = np.zeros_like(hi)
+    return np.concatenate([hi, blank, blank, hi, lo, blank, blank, lo], 1)
+
+
 def four_blocks(table):
     return np.kron(np.eye(4), table.astype(np.float32)).astype(table.dtype)
 
@@ -72,7 +77,7 @@
     zero = np.zeros((), ml_dtypes.bfloat16)
     order = np.array([4 * (r % 16) + r // 16 for r in range(NS)])
     y_syn = np.concatenate([short_hi, short_lo, short_hi, short_lo], 1)[order]
-    z_syn = np.concatenate([four_blocks(short_hi.T), four_blocks(short_lo.T)], 1)
+    z_syn = block_tiles(short_hi.T, short_lo.T)
     stacked = np.concatenate([hi, lo, hi, lo], 1)
     x_syn = np.full((SHARDS, 2, 12, 2, 128), zero)
     for half in range(2):
@@ -87,7 +92,7 @@
     x_ana = np.concatenate(parts, 0)
     z_ana = np.concatenate([four_blocks(short_hi), four_blocks(short_lo)], 1)
     y_ana = np.concatenate([np.concatenate([t[order].T] * 2, 1) for t in (short_hi, short_lo)], 0)
-    z_fit = np.concatenate([four_blocks(fit_hi.T), four_blocks(fit_lo.T)], 1)
+    z_fit = block_tiles(fit_hi.T, fit_lo.T)
     rows = np.array([2 * (r % 32) + r // 32 for r in range(NS)])
     columns = np.array([4 * (r % 24) + r // 24 for r in range(NG)])
     y_fit = np.concatenate([t[rows][:, columns] for t in (fit_hi, fit_lo, fit_hi, fit_lo)], 1)
@@ -132,6 +137,16 @@
     ah, al = split(a)
     wide = dot(ah, table[...])
     return wide[:, :width] + wide[:, width:] + dot(al, table[:, :width])
+
+
+def spread_blocks(tiles, table):
+    size = tiles.shape[0]
+    table[...] = jnp.zeros(table.shape, BF16)
+    for j in range(4):
+        for part in range(2):
+            column = 256 * part + 128 * (j // 2)
+            source = 128 * (2 * part + j % 2)
+            table[size * j : size * j + size, column : column + 128] = tiles[:, source : source + 128]
 
 
 def fit_potential(v_ref, tabs, planes, own):
@@ -240,7 +255,7 @@
     tabs = refs[12:20]
     scratch = refs[20:24]
     (v, planes, own, pack, coeffs, spread, landed, pairs, mate, gathered, blocks, relay, rotation_ref, left, rotated, local_sem,
-     a_send, a_recv, v_send, v_recv, b_send, b_recv, c_send, c_recv, news) = refs[24:]
+     fit_tiles, syn_tiles, a_send, a_recv, v_send, v_recv, b_send, b_recv, c_send, c_recv, news) = refs[24:]
     band = lax.axis_index("band")
     grid = lax.axis_index("grid")
     z_hi, y, core, chip = band // 8, (band // 2) % 4, band % 2, band // 2
@@ -263,12 +278,12 @@
         )
 
     sources = (v_hbm, tables_hbm[6], tables_hbm[7], x_hbm, rotation_hbm) + tuple(tables_hbm[:6])
-    targets = (v_ref, tabs[6], tabs[7], x_ref, rotation_ref) + tuple(tabs[:6])
+    targets = (v_ref, fit_tiles, tabs[7], x_ref, rotation_ref, tabs[0], syn_tiles) + tuple(tabs[2:6])
     fetches = [
         pltpu.make_async_copy(src, dst, local_sem.at[i])
         for i, (src, dst) in enumerate(zip(sources, targets))
     ]
-    for fetch in fetches:
+    for fetch in fetches[:3]:
         fetch.start()
 
     barrier = pltpu.get_barrier_semaphore()
@@ -276,6 +291,8 @@
     neighbours += [x_step(1), x_step(3), y_step(1), y_step(3), sibling]
     for to in neighbours:
         pl.semaphore_signal(barrier, inc=1, device_id=to, device_id_type=MESH)
+    for fetch in fetches[3:]:
+        fetch.start()
 
     def tell(turn):
         for to in (y_step(1), y_step(3)) if turn == 0 else (z_step(1), z_step(7)):
@@ -284,8 +301,10 @@
     def hear(turn):
         pl.semaphore_wait(news.at[turn], 2)
 
-    for fetch in fetches[:3]:
-        fetch.wait()
+    fetches[1].wait()
+    spread_blocks(fit_tiles, tabs[6])
+    fetches[0].wait()
+    fetches[2].wait()
     fit_potential(v_ref, tabs, planes, own)
     for column in range(2):
         v[column, grid] = own[192 * column : 192 * column + 192]
@@ -354,6 +373,7 @@
     inverse = 1.0 / ((upper[0] - lower[0]) * 0.5)
     for fetch in fetches[4:]:
         fetch.wait()
+    spread_blocks(syn_tiles, tabs[1])
     rh, rl = split(rotation_ref[...].T)
     left[...] = jnp.concatenate([rh, rl, rh, rl], 1)
     from_x(0, 1, 0)
@@ -572,6 +592,8 @@
         pltpu.VMEM((192, 256), BF16),
         pltpu.VMEM((192, 4096), F32),
         pltpu.SemaphoreType.DMA((11,)),
+        pltpu.VMEM((96, 512), BF16),
+        pltpu.VMEM((32, 512), BF16),
         pltpu.SemaphoreType.DMA((3,)),
         pltpu.SemaphoreType.DMA((3,)),
         pltpu.SemaphoreType.DMA((22,)),

time: 54.2 us -> 54.4 us (level)
  no operation moved by 1% of the time
where the time goes in v6:
time: 54.4 us; the launch traced here: 54.3 us
  Pallas kernels  52.3 us (96%)
  between operations  1.93 us (4%)
    pallas_call x1, Pallas kernels, body(): FILTER(block_coeffs, potential, coefficients, lower_edge, upper_edge, own...  49.5 us
    pallas_call x1, Pallas kernels, body(): WRITE(*FILTER(block_coeffs, potential, coefficients, lower_edge, upper_ed...  2.88 us

profile of v6, /device:TPU:1, one launch (start us, length us, event | category | flops | bytes accessed | tf_op | source)
XLA Modules:
  0.0 54.3 jit_solution(3827909781615802494)
XLA Ops:
  1.9 49.5 %filter.1 = (f32[8,4096]{1,0:T(8,128)}, f32[192,4096]{1,0:T(8,128)}) custom-call(f32[8,4096]{1,0:T(8,128)} %x_hbm.1, f32[12,9216]{1,0:T(8,128)} %v_hbm.1, f32[64,192]{1,0:T(8,128)} %bitcast.3, f32[1]{0:T(128)S(6)} %copy.16.lower, f32[1]{0:T(128)S(6)} %copy.17.upper, s32[8]{0:T(128)} %owners.1, bf16[64,128]{1,0:T(8,128)(2,1)} %constant.16.clone.refs_0_, ...), custom_call_target="tpu_custom_call" | custom-call | tf_op jit(solution)/shard_map/filter/pallas_call | solution.py:653
  51.4 2.9 %write.1 = (f32[8,4096]{1,0:T(8,128)}, f32[192,4096]{1,0:T(8,128)}) custom-call(f32[8,4096]{1,0:T(8,128)} %get-tuple-element.4.filtered, f32[192,4096]{1,0:T(8,128)} %get-tuple-element.5.residents), custom_call_target="tpu_custom_call" | custom-call | tf_op jit(solution)/shard_map/write/pallas_call | solution.py:653
